TPU v7x, 32 devices: a whole 2x2x4 slice. The times are simulated.
32 devices in a mesh: lat: 4 (over y, x), lon: 8 (over z, core).
Axes of the slice: x: 2, y: 2, z: 4, core: 2. Of those that a mesh axis runs over, the one named last changes fastest.
Arguments:
- height: float32 [768, 3072], P('lat', 'lon'), may hold values from -6 to 6
- flux_lon: float32 [768, 3072], P('lat', 'lon'), may hold values from -4 to 4
- flux_lat: float32 [768, 3072], P('lat', 'lon'), may hold values from -4 to 4
- depth: float32 [768, 3072], P('lat', 'lon'), may hold values from 0.05 to 1
- wet: int32 [768, 3072], P('lat', 'lon'), may hold values 0 or 1
- kernel: float32 [96, 96, 192], P('lat', None, 'lon'), may hold values from -0.5 to 0.5
Outputs:
- height_out: float32 [768, 3072], P('lat', 'lon')
- flux_lon_out: float32 [768, 3072], P('lat', 'lon')
- flux_lat_out: float32 [768, 3072], P('lat', 'lon')
- loading_out: float32 [96, 192], P('lat', 'lon')
All inputs are finite; a program needn't handle non-finite values. No bound on the sum of `wet` on one device may be relied on, other than what follows from the above.
Results may differ from a plain program's by a relative error of at most 0.00011.
Values sent between devices are 32-bit elements; how exact they have to be, the bound alone decides.
A program may use at most 128 MiB of HBM per device.

v0:
```python
import math

import jax
import jax.numpy as jnp
from jax import lax
from jax.sharding import PartitionSpec as P

CROWS = 24
CCOLS = 24
STEPS = 2
ROW_RATIO = 8
COL_RATIO = 16


angle_step = math.pi / (180.0 * 240.0)
courant_lon = 0.3
courant_lat = 0.3


def padded(cells, sides, width, closed):
    for axis, dim in sides:
        count = lax.axis_size(axis)
        ends = count if closed else count - 1
        head = lax.slice_in_dim(cells, 0, width, axis=dim)
        tail = lax.slice_in_dim(cells, cells.shape[dim] - width, cells.shape[dim], axis=dim)
        cells = jnp.concatenate(
            [
                lax.ppermute(tail, axis, [(i, (i + 1) % count) for i in range(ends)]),
                cells,
                lax.ppermute(head, axis, [((i + 1) % count, i) for i in range(ends)]),
            ],
            axis=dim,
        )
    return cells


def coslat(position, total):
    return jnp.cos((position - 0.5 * total) * angle_step)


def edge_cols(field):
    return jnp.concatenate([field[:, :1], field[:, -1:]], 1)


def edge_rows(field):
    return jnp.concatenate([field[:1], field[-1:]], 0)


def body(height, flux_lon, flux_lat, depth, wet, kernel):
    lat_count = lax.axis_size("lat")
    lon_count = lax.axis_size("lon")
    rows, cols = height.shape
    grid_rows = rows * lat_count
    mass_rows = kernel.shape[1]
    mass_cols = CCOLS * lon_count
    wetf = wet.astype(jnp.float32)
    global_rows = (lax.axis_index("lat") * rows + jnp.arange(rows, dtype=jnp.int32)).astype(
        jnp.float32
    )
    cos_center = coslat(global_rows + 0.5, grid_rows)[:, None]
    cos_north = coslat(global_rows + 1.0, grid_rows)[:, None]
    cos_south = coslat(global_rows, grid_rows)[:, None]
    offset = lax.axis_index("lon") * CCOLS

    def contract(total, piece, start):
        width = piece.shape[0]
        shifted = jnp.roll(piece, offset, axis=1)
        stacked = jnp.stack([jnp.roll(shifted, lagged, axis=1) for lagged in range(CCOLS)])
        weights = lax.dynamic_slice_in_dim(kernel, start, width, 1)
        return total + jnp.einsum("aje,ejx->ax", weights, stacked, precision=lax.Precision.HIGHEST)

    loading = jnp.zeros((CROWS, CCOLS), jnp.float32)
    for step_index in range(STEPS):
        weighted = height * wetf * cos_center
        mass = weighted.reshape(CROWS, ROW_RATIO, CCOLS, COL_RATIO).mean(axis=(1, 3))
        empty = jnp.zeros((CROWS, mass_cols), jnp.float32)
        everyone = lax.all_gather(mass[None], ("lat", "lon"), axis=0, tiled=True)
        whole = (
            everyone.reshape(lat_count, lon_count, CROWS, CCOLS)
            .transpose(0, 2, 1, 3)
            .reshape(mass_rows, mass_cols)
        )

        def band_term(band, total):
            first = band * CROWS
            return contract(total, lax.dynamic_slice_in_dim(whole, first, CROWS, 0), first)

        partial_sum = lax.fori_loop(0, lat_count, band_term, empty)
        loading = lax.psum_scatter(partial_sum, "lon", scatter_dimension=1, tiled=True)
        zeta = height + jnp.repeat(jnp.repeat(loading, ROW_RATIO, axis=0), COL_RATIO, axis=1)
        lon_edges = jnp.stack(
            [edge_cols(zeta), edge_cols(flux_lon), edge_cols(depth), edge_cols(wetf)]
        )
        lon_rim = padded(lon_edges, (("lon", 2),), 1, True)
        lat_edges = jnp.stack(
            [edge_rows(zeta), edge_rows(flux_lat), edge_rows(depth), edge_rows(wetf)]
        )
        lat_rim = padded(lat_edges, (("lat", 1),), 1, False)
        zeta_lon = jnp.concatenate([lon_rim[0, :, :1], zeta, lon_rim[0, :, 3:]], 1)
        depth_lon = jnp.concatenate([lon_rim[2, :, :1], depth, lon_rim[2, :, 3:]], 1)
        wet_lon = jnp.concatenate([lon_rim[3, :, :1], wetf, lon_rim[3, :, 3:]], 1)
        old_lon = jnp.concatenate([lon_rim[1, :, :1], flux_lon], 1)
        lon_faces = (
            wet_lon[:, :-1]
            * wet_lon[:, 1:]
            * (
                old_lon
                - courant_lon
                / cos_center
                * (0.5 * (depth_lon[:, :-1] + depth_lon[:, 1:]))
                * (zeta_lon[:, 1:] - zeta_lon[:, :-1])
            )
        )
        zeta_lat = jnp.concatenate([lat_rim[0, :1], zeta, lat_rim[0, 3:]], 0)
        depth_lat = jnp.concatenate([lat_rim[2, :1], depth, lat_rim[2, 3:]], 0)
        wet_lat = jnp.concatenate([lat_rim[3, :1], wetf, lat_rim[3, 3:]], 0)
        old_lat = jnp.concatenate([lat_rim[1, :1], flux_lat], 0)
        lat_faces = (
            wet_lat[:-1]
            * wet_lat[1:]
            * (
                old_lat
                - courant_lat
                * (0.5 * (depth_lat[:-1] + depth_lat[1:]))
                * (zeta_lat[1:] - zeta_lat[:-1])
            )
        )
        flux_lon = lon_faces[:, 1:]
        flux_lat = lat_faces[1:]
        height = wetf * (
            height
            - courant_lon / cos_center * (flux_lon - lon_faces[:, :-1])
            - courant_lat / cos_center * (cos_north * flux_lat - cos_south * lat_faces[:-1])
        )
    return (height, flux_lon, flux_lat, loading)


def solution(mesh):
    return jax.shard_map(
        body,
        mesh=mesh,
        in_specs=(
            P("lat", "lon"),
            P("lat", "lon"),
            P("lat", "lon"),
            P("lat", "lon"),
            P("lat", "lon"),
            P("lat", None, "lon"),
        ),
        out_specs=(P("lat", "lon"), P("lat", "lon"), P("lat", "lon"), P("lat", "lon")),
        check_vma=False,
    )
```

profile of v0, /device:TPU:0, one launch (start us, length us, event | category | flops | bytes accessed | tf_op | source)
XLA Modules:
  0.0 223.5 jit_solution(196296318080770362)
XLA Ops:
  0.7 1.1 copy.128
  1.8 1.1 copy.133
  3.0 1.1 copy.123
  4.7 2.2 reshape.78
  6.9 1.9 reduce_sum.18
  8.8 44.8 %all-gather = f32[768,24]{1,0:T(8,128)S(1)} all-gather(f32[24,24]{1,0:T(8,128)S(1)} %broadcast_multiply_fusion.1), channel_id=2, replica_groups=mesh['lat'=4,'lon'=8] {'lat','lon'}, dimensions={0}, use_global_device_ids=true | all-gather | bytes 76032 | tf_op jit(solution)/shard_map/all_gather | solution.py:77
  53.9 17.5 %while.28 = (s32[]{:T(128)}, f32[24,192]{1,0:T(8,128)S(1)}, f32[24,96,24]{1,0,2:T(8,128)S(1)}, f32[96,192]{1,0:T(8,128)S(1)}, s32[]{:T(128)}, /*index=5*/s32[]{:...) while((s32[]{:T(128)}, f32[24,192]{1,0:T(8,128)S(1)}, ...), condition=%wide.region_2.4_spmd.clone, body=%wide.region_1.3_spmd.clone.sunk | while | flops 31970320 | bytes 2271265 | solution.py:88
  71.4 26.1 %all-reduce = f32[24,192]{1,0:T(8,128)S(1)} all-reduce(f32[24,192]{1,0:T(8,128)S(1)} %get-tuple-element.193), channel_id=4, replica_groups=mesh['lat'=4,'lon'=8] {'lon'}, use_global_device_ids=true, to_apply=%region_3.5.clone | all-reduce | flops 4608 | bytes 36864
  101.9 1.3 collective-permute-start.3
  103.2 4.5 %collective-permute-start.2 = (f32[4,1,384]{2,0,1:T(4,128)S(1)}, f32[4,1,384]{2,0,1:T(4,128)S(1)}, u32[]{:S(2)}, u32[]{:S(2)}) collective-permute-start(f32[4,1,384]{2,0,1:T(4,128)S(1)} %get-tuple-element.355), channel_id=1, source_target_pairs={{0,8},{8,16},{16,24},{1,9},{9,17},{17,25},{2,10},{10,18},{18,26},{... | collective-permute-start | bytes 18440 | tf_op jit(solution)/shard_map/ppermute | solution.py:28
  107.9 1.1 copy.150
  109.6 0.8 copy.151
  110.5 0.8 copy.149
  111.3 0.8 copy.147
  112.9 0.8 copy.148
  113.8 1.9 fusion.26
  115.7 0.9 fusion.43
  116.6 1.1 multiply_multiply_fusion
  117.8 2.2 reshape.83
  120.0 1.9 reduce_sum.19
  121.9 38.9 %all-gather.1 = f32[768,24]{1,0:T(8,128)S(1)} all-gather(f32[24,24]{1,0:T(8,128)S(1)} %broadcast_multiply_fusion), channel_id=3, replica_groups=mesh['lat'=4,'lon'=8] {'lat','lon'}, dimensions={0}, use_global_device_ids=true | all-gather | bytes 76032 | tf_op jit(solution)/shard_map/all_gather | solution.py:77
  161.1 17.5 %while.29 = (s32[]{:T(128)}, f32[24,192]{1,0:T(8,128)S(1)}, f32[24,96,24]{1,0,2:T(8,128)S(1)}, f32[96,192]{1,0:T(8,128)S(1)}, s32[]{:T(128)}, /*index=5*/s32[]{:...) while((s32[]{:T(128)}, f32[24,192]{1,0:T(8,128)S(1)}, ...), condition=%wide.region_6.8_spmd.clone, body=%wide.region_5.7_spmd.clone.sunk | while | flops 31970320 | bytes 2271265 | solution.py:88
  178.6 26.3 %all-reduce.1 = f32[24,192]{1,0:T(8,128)S(1)} all-reduce(f32[24,192]{1,0:T(8,128)S(1)} %get-tuple-element.194), channel_id=5, replica_groups=mesh['lat'=4,'lon'=8] {'lon'}, use_global_device_ids=true, to_apply=%region_7.9.clone | all-reduce | flops 4608 | bytes 36864
  206.6 1.0 copy.164
  207.8 1.3 collective-permute-start.7
  209.1 4.5 %collective-permute-start.6 = (f32[4,1,384]{2,0,1:T(4,128)S(1)}, f32[4,1,384]{2,0,1:T(4,128)S(1)}, u32[]{:S(2)}, u32[]{:S(2)}) collective-permute-start(f32[4,1,384]{2,0,1:T(4,128)S(1)} %get-tuple-element.353), channel_id=1, source_target_pairs={{0,8},{8,16},{16,24},{1,9},{9,17},{17,25},{2,10},{10,18},{18,26},{... | collective-permute-start | bytes 18440 | tf_op jit(solution)/shard_map/ppermute | solution.py:28
  214.0 1.0 collective-permute-done.6
  215.5 0.8 copy.174
  218.8 1.8 fusion.29
  221.0 0.9 copy.182
  221.8 0.9 copy.181
  222.7 0.9 copy.183
  (506 shorter events, 46.0 us)
Async XLA Ops:
  0.6 3.5 %copy-start.3 = (f32[192,384]{1,0:T(8,128)S(1)}, f32[192,384]{1,0:T(8,128)}, u32[]{:S(2)}) copy-start(f32[192,384]{1,0:T(8,128)} %param.12) | copy-start | bytes 884740
  0.6 3.7 %copy-start.4 = (f32[192,384]{1,0:T(8,128)S(1)}, f32[192,384]{1,0:T(8,128)}, u32[]{:S(2)}) copy-start(f32[192,384]{1,0:T(8,128)} %param.13) | copy-start | bytes 884740
  53.9 43.6 %copy-start.6 = (u32[32]{0:T(128)S(1)}, u32[32]{0:T(128)}, u32[]{:S(2)}) copy-start(u32[32]{0:T(128)} %constant.115) | copy-start | bytes 388
  99.0 10.0 %collective-permute-start.1 = (f32[4,192,1]{1,2,0:T(1,128)S(1)}, f32[4,192,1]{1,2,0:T(1,128)S(1)}, u32[]{:S(2)}, u32[]{:S(2)}) collective-permute-start(f32[4,192,1]{1,2,0:T(1,128)S(1)} %get-tuple-element.358), channel_id=1, source_target_pairs={{1,0},{2,1},{3,2},{4,3},{5,4},{6,5},{7,6},{0,7},{9,8},{10,9},{11,1... | collective-permute-start | bytes 9224 | tf_op jit(solution)/shard_map/ppermute | solution.py:30
  99.1 9.9 %collective-permute-start = (f32[4,192,1]{1,2,0:T(1,128)S(1)}, f32[4,192,1]{1,2,0:T(1,128)S(1)}, u32[]{:S(2)}, u32[]{:S(2)}) collective-permute-start(f32[4,192,1]{1,2,0:T(1,128)S(1)} %get-tuple-element.359), channel_id=1, source_target_pairs={{0,1},{1,2},{2,3},{3,4},{4,5},{5,6},{6,7},{7,0},{8,9},{9,10},{10,1... | collective-permute-start | bytes 9224 | tf_op jit(solution)/shard_map/ppermute | solution.py:28
  101.9 7.6 %collective-permute-start.3 = (f32[4,1,384]{2,0,1:T(4,128)S(1)}, f32[4,1,384]{2,0,1:T(4,128)S(1)}, u32[]{:S(2)}, u32[]{:S(2)}) collective-permute-start(f32[4,1,384]{2,0,1:T(4,128)S(1)} %get-tuple-element.354), channel_id=1, source_target_pairs={{8,0},{16,8},{24,16},{9,1},{17,9},{25,17},{10,2},{18,10},{26,18},{... | collective-permute-start | bytes 18440 | tf_op jit(solution)/shard_map/ppermute | solution.py:30
  103.2 6.1 %collective-permute-start.2 = (f32[4,1,384]{2,0,1:T(4,128)S(1)}, f32[4,1,384]{2,0,1:T(4,128)S(1)}, u32[]{:S(2)}, u32[]{:S(2)}) collective-permute-start(f32[4,1,384]{2,0,1:T(4,128)S(1)} %get-tuple-element.355), channel_id=1, source_target_pairs={{0,8},{8,16},{16,24},{1,9},{9,17},{17,25},{2,10},{10,18},{18,26},{... | collective-permute-start | bytes 18440 | tf_op jit(solution)/shard_map/ppermute | solution.py:28
  161.0 44.7 %copy-start.2 = (f32[1,384]{0,1:T(8,128)S(1)}, f32[1,384]{0,1:T(8,128)}, u32[]{:S(2)}) copy-start(f32[1,384]{0,1:T(8,128)} %get-tuple-element.342) | copy-start | bytes 4612
  161.1 44.8 %copy-start.1 = (f32[1,384]{0,1:T(8,128)S(1)}, f32[1,384]{0,1:T(8,128)}, u32[]{:S(2)}) copy-start(f32[1,384]{0,1:T(8,128)} %get-tuple-element.343) | copy-start | bytes 4612
  178.6 35.2 %copy-start = (f32[192,384]{0,1:T(8,128)S(1)}, f32[192,384]{0,1:T(8,128)}, u32[]{:S(2)}) copy-start(f32[192,384]{0,1:T(8,128)} %get-tuple-element.325) | copy-start | bytes 884740
  204.9 9.1 %copy-start.5 = (f32[24,24]{1,0:T(8,128)}, f32[24,24]{1,0:T(8,128)S(1)}, u32[]{:S(2)}) copy-start(f32[24,24]{1,0:T(8,128)S(1)} %constant_dynamic-slice_fusion.2) | copy-start | bytes 6916
  206.1 7.6 %collective-permute-start.5 = (f32[4,192,1]{1,2,0:T(1,128)S(1)}, f32[4,192,1]{1,2,0:T(1,128)S(1)}, u32[]{:S(2)}, u32[]{:S(2)}) collective-permute-start(f32[4,192,1]{1,2,0:T(1,128)S(1)} %get-tuple-element.356), channel_id=1, source_target_pairs={{1,0},{2,1},{3,2},{4,3},{5,4},{6,5},{7,6},{0,7},{9,8},{10,9},{11,1... | collective-permute-start | bytes 9224 | tf_op jit(solution)/shard_map/ppermute | solution.py:30
  206.1 7.6 %collective-permute-start.4 = (f32[4,192,1]{1,2,0:T(1,128)S(1)}, f32[4,192,1]{1,2,0:T(1,128)S(1)}, u32[]{:S(2)}, u32[]{:S(2)}) collective-permute-start(f32[4,192,1]{1,2,0:T(1,128)S(1)} %get-tuple-element.357), channel_id=1, source_target_pairs={{0,1},{1,2},{2,3},{3,4},{4,5},{5,6},{6,7},{7,0},{8,9},{9,10},{10,1... | collective-permute-start | bytes 9224 | tf_op jit(solution)/shard_map/ppermute | solution.py:28
  207.8 7.3 %collective-permute-start.7 = (f32[4,1,384]{2,0,1:T(4,128)S(1)}, f32[4,1,384]{2,0,1:T(4,128)S(1)}, u32[]{:S(2)}, u32[]{:S(2)}) collective-permute-start(f32[4,1,384]{2,0,1:T(4,128)S(1)} %get-tuple-element.352), channel_id=1, source_target_pairs={{8,0},{16,8},{24,16},{9,1},{17,9},{25,17},{10,2},{18,10},{26,18},{... | collective-permute-start | bytes 18440 | tf_op jit(solution)/shard_map/ppermute | solution.py:30
  209.1 5.9 %collective-permute-start.6 = (f32[4,1,384]{2,0,1:T(4,128)S(1)}, f32[4,1,384]{2,0,1:T(4,128)S(1)}, u32[]{:S(2)}, u32[]{:S(2)}) collective-permute-start(f32[4,1,384]{2,0,1:T(4,128)S(1)} %get-tuple-element.353), channel_id=1, source_target_pairs={{0,8},{8,16},{16,24},{1,9},{9,17},{17,25},{2,10},{10,18},{18,26},{... | collective-permute-start | bytes 18440 | tf_op jit(solution)/shard_map/ppermute | solution.py:28
where the time goes:
time: 225 us; the launch traced here: 224 us
  blocking collectives  136 us (60%)
  local copies, waits for them, and re-layouts  40 us (18%)
  other arithmetic  24.9 us (11%)
  starting transfers between devices  12.8 us (6%)
  matrix products  5.94 us (3%)
    all_gather x2, blocking collectives, body(): everyone = lax.all_gather(mass[None], ('lat', 'lon'), axis=0, tiled=True)  83.7 us
    unnamed x2, blocking collectives  52.4 us
    while x184, other arithmetic  14.4 us
    slice x184, local copies, waits for them, and re-layouts, contract(): jnp.roll(shifted, lagged, axis=1)  13.3 us
    ppermute x4, starting transfers between devices, padded(): lax.ppermute(tail, axis, [(i, (i + 1) % count) for i in range(ends)])  10.1 us
    unnamed x26, local copies, waits for them, and re-layouts  8.14 us
    dot_general x8, matrix products, contract(): jnp.einsum('aje,ejx->ax', weights, stacked, precision=lax.Precision.HIGHEST)  5.94 us
    slice x14, local copies, waits for them, and re-layouts, edge_rows(): return jnp.concatenate([field[:1], field[-1:]], 0)  5.04 us
  transfers between devices with their start and end apart: 8, of which 1 were waited for; matrix products, arithmetic and copies ran while one was open for 2% of the time, Pallas kernels for 0%

commit v1 on v0

v1 whole, which is shorter than its diff:
```python
import functools
import math

import jax
import jax.numpy as jnp
from jax import lax
from jax.experimental import pallas as pl
from jax.experimental.pallas import tpu as pltpu
from jax.sharding import PartitionSpec as P

STEPS = 2
ANGLE_STEP = math.pi / (180.0 * 240.0)
COURANT_LON = 0.3
COURANT_LAT = 0.3
MESH = pl.DeviceIdType.MESH
LANES = 128
SUB = 8
F32 = jnp.float32
BF16 = jnp.bfloat16


def up(value, unit):
    return -(-value // unit) * unit


def lane_of(shape):
    return lax.broadcasted_iota(jnp.int32, shape, len(shape) - 1)


def sub_of(shape):
    return lax.broadcasted_iota(jnp.int32, shape, len(shape) - 2)


def turn(cells, shift, axis):
    shift = shift % cells.shape[axis]
    return cells if shift == 0 else pltpu.roll(cells, shift, axis)


def take(cells, start, width, dest):
    first, offset = start // LANES, start % LANES
    head = turn(cells[:, first * LANES : (first + 1) * LANES], dest - offset, 1)
    if offset + width <= LANES:
        return head
    tail = turn(cells[:, (first + 1) * LANES : (first + 2) * LANES], dest - offset, 1)
    return jnp.where(lane_of(head.shape) < dest + LANES - offset, head, tail)


def halves(cells):
    high = cells.astype(BF16)
    return high, (cells - high.astype(F32)).astype(BF16)


def exact_dot(cells, picks):
    high = cells.astype(BF16).astype(F32)
    rest = cells - high
    middle = rest.astype(BF16).astype(F32)
    terms = jnp.concatenate([high, middle, rest - middle], 0).astype(BF16)
    summed = jnp.dot(terms, picks, preferred_element_type=F32)
    rows = cells.shape[0]
    return summed[:rows] + (summed[rows : 2 * rows] + summed[2 * rows :])


def run(
    lat_n, lon_n,
    height, flux_lon, flux_lat, depth, wet, kernel,
    out_height, out_lon, out_lat, out_loading,
    field, wet_in, kin, state, final, coef, rowc, zeta, gather_m, expand_m,
    kt, khi, klo, mslot, mass_all, psend, precv,
    lonh_send, lonh_recv, lath_send, lath_recv,
    in_sem, out_sem, mass_ss, mass_rs, all_ss, all_rs, part_ss, part_rs,
    kh_ss, kh_rs, lonh_ss, lonh_rs, lath_ss, lath_rs,
):
    lat, lon = lax.axis_index("lat"), lax.axis_index("lon")
    rows, cols = height.shape
    crows, ccols, jrows = kernel.shape
    all_rows, all_cols = field.shape[1:]
    tiles = all_rows // SUB
    jpad = up(jrows, LANES)
    width = mass_all.shape[2]
    north, south = lax.rem(lat + 1, lat_n), lax.rem(lat + lat_n - 1, lat_n)
    east, west = lax.rem(lon + 1, lon_n), lax.rem(lon + lon_n - 1, lon_n)
    lon_peer = [lax.rem(lon + off, lon_n) for off in range(lon_n)]
    lat_peer = [lax.rem(lat + off, lat_n) for off in range(lat_n)]

    def send(src, dst, ss, rs, to):
        copy = pltpu.make_async_remote_copy(
            src_ref=src, dst_ref=dst, send_sem=ss, recv_sem=rs, device_id=to, device_id_type=MESH
        )
        copy.start()
        return copy

    own = (pl.ds(0, rows), pl.ds(0, cols))
    loads = [
        pltpu.make_async_copy(height, field.at[(0, *own)], in_sem.at[0]),
        pltpu.make_async_copy(wet, wet_in, in_sem.at[4]),
        pltpu.make_async_copy(flux_lon, field.at[(1, *own)], in_sem.at[1]),
        pltpu.make_async_copy(flux_lat, field.at[(2, *own)], in_sem.at[2]),
        pltpu.make_async_copy(depth, field.at[(3, *own)], in_sem.at[3]),
        pltpu.make_async_copy(kernel, kin.at[pl.ds(0, crows)], in_sem.at[5]),
    ]
    for copy in loads:
        copy.start()
    barrier = pltpu.get_barrier_semaphore()
    for off in range(1, lon_n):
        pl.semaphore_signal(barrier, inc=1, device_id=(lat, lon_peer[off]), device_id_type=MESH)
    for off in range(1, lat_n):
        pl.semaphore_signal(barrier, inc=1, device_id=(lat_peer[off], lon), device_id_type=MESH)

    place = sub_of((all_rows, LANES))
    place = jnp.where(place >= all_rows - SUB // 2, place - all_rows, place) + lat * rows
    place = place.astype(F32)

    def coslat(position):
        return jnp.cos((position - 0.5 * (rows * lat_n)) * ANGLE_STEP)

    cos_center = coslat(place + 0.5)
    rowc[0] = cos_center
    rowc[1] = COURANT_LON / cos_center
    rowc[2] = COURANT_LAT / cos_center * coslat(place + 1.0)
    rowc[3] = COURANT_LAT / cos_center * coslat(place)
    row_ratio, col_ratio = rows // crows, cols // ccols
    gather_m[...] = jnp.where(
        lax.broadcasted_iota(jnp.int32, (cols, LANES), 0) // col_ratio == lane_of((cols, LANES)),
        1.0 / (row_ratio * col_ratio),
        0.0,
    ).astype(BF16)
    fine = lane_of((LANES, all_cols))
    fine = jnp.where(fine < cols + LANES // 2, 1 + fine // col_ratio, 0)
    expand_m[...] = jnp.where(sub_of((LANES, all_cols)) == fine, 1.0, 0.0).astype(BF16)

    def wide(cells, count):
        return jnp.concatenate([cells] * count, 1)

    def send_mass(step, level):
        weighted = level * field[4, :rows, :cols] * wide(rowc[0, :rows], cols // LANES)
        summed = weighted.reshape(crows, row_ratio, cols).sum(axis=1)
        mass = exact_dot(summed, gather_m[...])
        lanes = lane_of((SUB, LANES))
        packed = mass[:SUB]
        for part in range(1, crows // SUB):
            moved = turn(mass[part * SUB : (part + 1) * SUB], 32 * part, 1)
            packed = jnp.where(lanes >= 32 * part, moved, packed)
        mslot[step, lon] = packed
        if step == 0:
            pl.semaphore_wait(barrier, lon_n + lat_n - 2)
        return [
            send(
                mslot.at[step, lon], mslot.at[step, lon],
                mass_ss.at[step, off], mass_rs.at[step, off], (lat, lon_peer[off]),
            )
            for off in range(1, lon_n)
        ]

    def send_band(step, copies):
        for copy in copies:
            copy.wait_recv()
        lanes = lane_of((SUB, LANES))
        bands = []
        for part in range(crows // SUB):
            pieces = [jnp.zeros((SUB, LANES), F32) for _ in range(width // LANES)]
            for block in range(-(-width // ccols)):
                first = ccols * block
                slot = mslot[step, (block - 1) % lon_n]
                moved = turn(slot, first - 32 * part, 1)
                low, begin = first // LANES, first % LANES
                pieces[low] = jnp.where(lanes >= begin, moved, pieces[low])
                if begin + ccols > LANES and low + 1 < width // LANES:
                    pieces[low + 1] = moved
            bands.append(jnp.concatenate(pieces, 1))
        here = pl.ds(pl.multiple_of(lat * crows, SUB), crows)
        mass_all[step, here] = jnp.concatenate(bands, 0)
        return [
            send(
                mass_all.at[step, here], mass_all.at[step, here],
                all_ss.at[step, off], all_rs.at[step, off], (lat_peer[off], lon),
            )
            for off in range(1, lat_n)
        ]

    def send_partials(step, copies):
        for copy in copies:
            copy.wait_recv()
        mass = mass_all[step]
        both = [mass, turn(mass, ccols // 2, 1)]
        if jpad > jrows:
            blank = jnp.zeros((jpad - jrows, width), F32)
            both = [both[0], blank, both[1], blank]
        high, low = halves(jnp.concatenate(both, 0))
        left = khi[...]
        product = (
            jnp.dot(left, high, preferred_element_type=F32)
            + jnp.dot(klo[...], high, preferred_element_type=F32)
            + jnp.dot(left, low, preferred_element_type=F32)
        )
        lags, shift = ccols // 2, 1
        product = product.reshape(lags, 32, width)
        while lags % 2 == 0:
            product = product.reshape(lags // 2, 2, 32, width)
            lags //= 2
            moved = turn(product[:, 1].reshape(lags * 32, width), shift, 1)
            product = product[:, 0] + moved.reshape(lags, 32, width)
            shift *= 2
        total = product[0]
        for lag in range(1, lags):
            total = total + turn(product[lag], shift * lag, 1)
        lanes = lane_of((SUB, LANES))
        sent = []
        for off in range(lon_n):
            packed = None
            for part in range(4):
                got = take(
                    total[part * SUB : (part + 1) * SUB], ccols * (off + 1) - 1, ccols + 2, 32 * part
                )
                packed = got if part == 0 else jnp.where(lanes >= 32 * part, got, packed)
            if off == 0:
                precv[step, 0] = packed
            else:
                psend[step, off] = packed
                sent.append(
                    send(
                        psend.at[step, off], precv.at[step, off],
                        part_ss.at[step, off], part_rs.at[step, off], (lat, lon_peer[off]),
                    )
                )
        return sent

    def loading_of(step, copies):
        for copy in copies:
            copy.wait_recv()
        total = precv[step, 0]
        for off in range(1, lon_n):
            total = total + precv[step, off]
        return jnp.concatenate([turn(total, -32 * part, 1) for part in range(4)], 0)

    def set_zeta(level, loading):
        spread = exact_dot(loading, expand_m[...])
        sub = sub_of((SUB, all_cols))
        for tile in range(tiles):
            rise = jnp.broadcast_to(spread[tile : tile + 1], (SUB, all_cols))
            if tile == tiles - 1:
                below = jnp.broadcast_to(spread[tile + 1 : tile + 2], (SUB, all_cols))
                rise = jnp.where(sub < SUB // 2, rise, below)
            at = pl.ds(tile * SUB, SUB)
            zeta[at, :] = level[at, :] + rise

    def advance(level, old_lon, old_lat, new):
        sub = sub_of((SUB, all_cols))

        def one(turn_index, below):
            here = lax.rem(turn_index + tiles - 1, tiles)
            after = lax.rem(turn_index, tiles)
            at = pl.ds(pl.multiple_of(here * SUB, SUB), SUB)
            up_at = pl.ds(pl.multiple_of(after * SUB, SUB), SUB)
            z = zeta[at, :]
            z_north = turn(jnp.where(sub == 0, zeta[up_at, :], z), SUB - 1, 0)
            z_east = turn(z, all_cols - 1, 1)
            lon_new = coef[1, at, :] * old_lon[at, :] - coef[0, at, :] * (z_east - z)
            lat_new = coef[3, at, :] * old_lat[at, :] - coef[2, at, :] * (z_north - z)
            lat_south = turn(jnp.where(sub == SUB - 1, below, lat_new), 1, 0)
            count = all_cols // LANES
            new[1, at, :] = lon_new
            new[2, at, :] = lat_new
            new[0, at, :] = field[4, at, :] * (
                level[at, :]
                - wide(rowc[1, at, :], count) * (lon_new - turn(lon_new, 1, 1))
                - (
                    wide(rowc[2, at, :], count) * lat_new
                    - wide(rowc[3, at, :], count) * lat_south
                )
            )
            return lat_new

        lax.fori_loop(0, tiles + 1, one, jnp.zeros((SUB, all_cols), F32))

    loads[0].wait()
    loads[1].wait()
    field[4, :rows, :cols] = wet_in[...].astype(F32)
    mass_copies = send_mass(0, field[0, :rows, :cols])
    pending = list(mass_copies)

    for copy in loads[2:5]:
        copy.wait()
    lanes = lane_of((rows, LANES))
    edges = jnp.zeros((rows, LANES), F32)
    for index in range(5):
        right = turn(field[index, :rows, cols - LANES : cols], 2 + 2 * index, 1)
        left = turn(field[index, :rows, :LANES], 16 + 2 * index, 1)
        edges = jnp.where(lanes // 2 == index, right, edges)
        edges = jnp.where(lanes // 2 == 8 + index, left, edges)
    square = lonh_send.shape[2]
    edges = jnp.concatenate([edges, jnp.zeros((square - rows, LANES), F32)], 0).T
    lonh_send[0] = edges[:16]
    lonh_send[1] = edges[16:32]
    lonh_copies = [
        send(lonh_send.at[0], lonh_recv.at[0], lonh_ss.at[0], lonh_rs.at[0], (lat, east)),
        send(lonh_send.at[1], lonh_recv.at[1], lonh_ss.at[1], lonh_rs.at[1], (lat, west)),
    ]
    pending += lonh_copies

    loads[5].wait()
    kh_copies = [
        send(kin.at[0], kin.at[crows], kh_ss.at[0], kh_rs.at[0], (south, lon)),
        send(kin.at[crows - 1], kin.at[crows + 1], kh_ss.at[1], kh_rs.at[1], (north, lon)),
    ]
    pending += kh_copies
    kt[...] = jnp.zeros(kt.shape, F32)

    band_copies = send_band(0, mass_copies)
    pending += band_copies

    half = ccols // 2
    for copy in kh_copies:
        copy.wait_recv()

    def one_row(row, carry):
        cells = kin[row]
        if jpad > jrows:
            cells = jnp.concatenate([cells, jnp.zeros((ccols, jpad - jrows), F32)], 1)
        for part in range(2):
            for chunk in range(jpad // LANES):
                piece = cells[part * half : (part + 1) * half, chunk * LANES : (chunk + 1) * LANES]
                kt[part * (jpad // LANES) + chunk, pl.ds(row, half, stride=32), :] = piece
        return carry

    lax.fori_loop(0, crows + 2, one_row, 0)
    for chunk in range(kt.shape[0]):
        high, low = halves(kt[chunk])
        khi[:, chunk * LANES : (chunk + 1) * LANES] = high
        klo[:, chunk * LANES : (chunk + 1) * LANES] = low

    part_copies = send_partials(0, band_copies)
    pending += part_copies

    for copy in lonh_copies:
        copy.wait_recv()
    arrived = jnp.concatenate(
        [lonh_recv[0], lonh_recv[1], jnp.zeros((LANES - 32, square), F32)], 0
    ).T[:rows]
    for index in range(5):
        from_west = turn(arrived, LANES - 2 - 2 * index, 1)
        from_east = turn(arrived, -16 - 2 * index, 1)
        field[index, :rows, cols:] = jnp.where(lanes < LANES // 2, from_east, from_west)
    sub = sub_of((SUB, all_cols))
    for side in range(2):
        packs = [jnp.zeros((SUB, all_cols), F32), jnp.zeros((SUB, all_cols), F32)]
        for index in range(5):
            if side == 0:
                edge = turn(field[index, rows - SUB : rows, :], 2 + 2 * index, 0)
            else:
                edge = turn(field[index, :SUB, :], 2 * index, 0)
            packs[index // 4] = jnp.where(sub // 2 == index % 4, edge, packs[index // 4])
        lath_send[side] = jnp.concatenate(packs, 0)
    lath_copies = [
        send(lath_send.at[0], lath_recv.at[0], lath_ss.at[0], lath_rs.at[0], (north, lon)),
        send(lath_send.at[1], lath_recv.at[1], lath_ss.at[1], lath_rs.at[1], (south, lon)),
    ]
    pending += lath_copies
    for copy in lath_copies:
        copy.wait_recv()
    for index in range(5):
        part = pl.ds(SUB * (index // 4), SUB)
        from_south = turn(lath_recv[0, part, :], 6 - 2 * index, 0)
        from_north = turn(lath_recv[1, part, :], -2 * index, 0)
        if index == 4:
            from_south = jnp.where(lat == 0, 0.0, 1.0) * from_south
            from_north = jnp.where(lat == lat_n - 1, 0.0, 1.0) * from_north
        field[index, rows:, :] = jnp.where(sub < SUB // 2, from_north, from_south)

    def factors(here, carry):
        after = lax.rem(here + 1, tiles)
        at = pl.ds(pl.multiple_of(here * SUB, SUB), SUB)
        up_at = pl.ds(pl.multiple_of(after * SUB, SUB), SUB)
        deep, sea = field[3, at, :], field[4, at, :]
        deep_north = turn(jnp.where(sub == 0, field[3, up_at, :], deep), SUB - 1, 0)
        sea_north = turn(jnp.where(sub == 0, field[4, up_at, :], sea), SUB - 1, 0)
        both = sea * turn(sea, all_cols - 1, 1)
        coef[1, at, :] = both
        coef[0, at, :] = (
            both
            * wide(rowc[1, at, :], all_cols // LANES)
            * (0.5 * (deep + turn(deep, all_cols - 1, 1)))
        )
        both = sea * sea_north
        coef[3, at, :] = both
        coef[2, at, :] = both * (COURANT_LAT * 0.5) * (deep + deep_north)
        return carry

    lax.fori_loop(0, tiles, factors, 0)

    set_zeta(field.at[0], loading_of(0, part_copies))
    advance(field.at[0], field.at[1], field.at[2], state)

    mass_copies = send_mass(1, state[0, :rows, :cols])
    band_copies = send_band(1, mass_copies)
    part_copies = send_partials(1, band_copies)
    pending += mass_copies + band_copies + part_copies
    loading = loading_of(1, part_copies)
    set_zeta(state.at[0], loading)
    advance(state.at[0], state.at[1], state.at[2], final)
    results = [
        pltpu.make_async_copy(final.at[(index, *own)], out, out_sem.at[index])
        for index, out in enumerate((out_height, out_lon, out_lat))
    ]
    for copy in results:
        copy.start()
    out_loading[...] = turn(loading[:crows], -1, 1)[:, :ccols]
    for copy in pending:
        copy.wait_send()
    for copy in results:
        copy.wait()


def body(height, flux_lon, flux_lat, depth, wet, kernel):
    lat_n, lon_n = lax.axis_size("lat"), lax.axis_size("lon")
    rows, cols = height.shape
    kernel = kernel.transpose(0, 2, 1)
    crows, ccols, jrows = kernel.shape
    all_rows, all_cols = rows + SUB, cols + LANES
    jpad = up(jrows, LANES)
    width = up(ccols * lon_n + ccols + 1, LANES)
    square = up(rows, LANES)
    lags = 32 * ccols // 2
    dma = pltpu.SemaphoreType.DMA
    block = jax.ShapeDtypeStruct((rows, cols), F32)
    anywhere = pl.BlockSpec(memory_space=pl.ANY)
    return pl.pallas_call(
        functools.partial(run, lat_n, lon_n),
        out_shape=[block, block, block, jax.ShapeDtypeStruct((crows, ccols), F32)],
        in_specs=[anywhere] * 6,
        out_specs=[anywhere] * 3 + [pl.BlockSpec(memory_space=pltpu.VMEM)],
        scratch_shapes=[
            pltpu.VMEM((5, all_rows, all_cols), F32),
            pltpu.VMEM((rows, cols), jnp.int32),
            pltpu.VMEM((crows + 2, ccols, jrows), F32),
            pltpu.VMEM((3, all_rows, all_cols), F32),
            pltpu.VMEM((3, all_rows, all_cols), F32),
            pltpu.VMEM((4, all_rows, all_cols), F32),
            pltpu.VMEM((4, all_rows, LANES), F32),
            pltpu.VMEM((all_rows, all_cols), F32),
            pltpu.VMEM((cols, LANES), BF16),
            pltpu.VMEM((LANES, all_cols), BF16),
            pltpu.VMEM((2 * jpad // LANES, lags, LANES), F32),
            pltpu.VMEM((lags, 2 * jpad), BF16),
            pltpu.VMEM((lags, 2 * jpad), BF16),
            pltpu.VMEM((STEPS, lon_n, SUB, LANES), F32),
            pltpu.VMEM((STEPS, jrows, width), F32),
            pltpu.VMEM((STEPS, lon_n, SUB, LANES), F32),
            pltpu.VMEM((STEPS, lon_n, SUB, LANES), F32),
            pltpu.VMEM((2, 16, square), F32),
            pltpu.VMEM((2, 16, square), F32),
            pltpu.VMEM((2, 16, all_cols), F32),
            pltpu.VMEM((2, 16, all_cols), F32),
            dma((6,)),
            dma((3,)),
            dma((STEPS, lon_n)),
            dma((STEPS, lon_n)),
            dma((STEPS, lat_n)),
            dma((STEPS, lat_n)),
            dma((STEPS, lon_n)),
            dma((STEPS, lon_n)),
            dma((2,)),
            dma((2,)),
            dma((2,)),
            dma((2,)),
            dma((2,)),
            dma((2,)),
        ],
        compiler_params=pltpu.CompilerParams(
            collective_id=0, has_side_effects=True, vmem_limit_bytes=40 * 2**20
        ),
    )(height, flux_lon, flux_lat, depth, wet, kernel)


def solution(mesh):
    return jax.shard_map(
        body,
        mesh=mesh,
        in_specs=(P("lat", "lon"),) * 5 + (P("lat", None, "lon"),),
        out_specs=(P("lat", "lon"),) * 4,
        check_vma=False,
    )
```

time: 225 us -> 50.5 us (0.22)
  blocking collectives: 136 us -> 0 us
  Pallas kernels: 0 us -> 41 us
  local copies, waits for them, and re-layouts: 40 us -> 8.5 us
  other arithmetic: 24.9 us -> 0 us
  starting transfers between devices: 12.8 us -> 0 us
  matrix products: 5.94 us -> 0 us
    all_gather x2 -> x0, blocking collectives: 83.7 us -> none  [body(): everyone = lax.all_gather(mass[None], ('lat', 'lon'), axis=0, tiled=True)]
    unnamed x2 -> x0, blocking collectives: 52.4 us -> none
    pallas_call x0 -> x1, Pallas kernels: none -> 41 us  [body(): pl.pallas_call(functools.partial(run, lat_n, lon_n), out_shape=[block, bl...]
    slice x208 -> x0, local copies, waits for them, and re-layouts: 18.4 us -> none  [the longest x184 13.3 us: contract(): jnp.roll(shifted, lagged, axis=1)]
    while x184 -> x0, other arithmetic: 14.4 us -> none
    ppermute x8 -> x0, starting transfers between devices: 12.8 us -> none  [the longest x4 10.1 us: padded(): lax.ppermute(tail, axis, [(i, (i + 1) % count) for i in range(ends)])]
    squeeze x22 -> x0, local copies, waits for them, and re-layouts: 8.14 us -> none  [the longest x4 3.3 us: body(): wet_lat = jnp.concatenate([lat_rim[3, :1], wetf, lat_rim[3, 3:]], 0)]
    dot_general x8 -> x0, matrix products: 5.94 us -> none  [contract(): jnp.einsum('aje,ejx->ax', weights, stacked, precision=lax.Precision.HIGHEST)]
  transfers between devices with their start and end apart: 8 -> 0, of which waited for: 1 -> 0; matrix products, arithmetic and copies ran while one was open for 2% -> 0% of each run, Pallas kernels for 0% -> 0%
where the time goes in v1:
time: 50.5 us; the launch traced here: 50.2 us
  Pallas kernels  41 us (81%)
  local copies, waits for them, and re-layouts  8.5 us (17%)
  between operations  0.66 us (1%)
    pallas_call x1, Pallas kernels, body(): pl.pallas_call(functools.partial(run, lat_n, lon_n), out_shape=[block, bl...  41 us
    unnamed x16, local copies, waits for them, and re-layouts  8.5 us

profile of v1, /device:TPU:0, one launch (start us, length us, event | category | flops | bytes accessed | tf_op | source)
XLA Modules:
  0.0 50.2 jit_solution(15096771211912664945)
XLA Ops:
  0.6 0.0 copy-start
  0.6 1.0 %copy-done = f32[192,384]{1,0:T(8,128)S(1)} copy-done((f32[192,384]{1,0:T(8,128)S(1)}, f32[192,384]{1,0:T(8,128)}, u32[]{:S(2)}) %copy-start) | copy-done | bytes 294936
  1.6 0.0 copy-start.1
  1.6 1.0 %copy-done.1 = f32[192,384]{1,0:T(8,128)S(1)} copy-done((f32[192,384]{1,0:T(8,128)S(1)}, f32[192,384]{1,0:T(8,128)}, u32[]{:S(2)}) %copy-start.1) | copy-done | bytes 294936
  2.6 0.0 copy-start.2
  2.6 1.0 %copy-done.2 = f32[192,384]{1,0:T(8,128)S(1)} copy-done((f32[192,384]{1,0:T(8,128)S(1)}, f32[192,384]{1,0:T(8,128)}, u32[]{:S(2)}) %copy-start.2) | copy-done | bytes 294936
  3.5 0.0 copy-start.3
  3.5 1.0 %copy-done.3 = f32[192,384]{1,0:T(8,128)S(1)} copy-done((f32[192,384]{1,0:T(8,128)S(1)}, f32[192,384]{1,0:T(8,128)}, u32[]{:S(2)}) %copy-start.3) | copy-done | bytes 294936
  4.5 0.0 copy-start.4
  4.5 1.0 %copy-done.4 = s32[192,384]{1,0:T(8,128)S(1)} copy-done((s32[192,384]{1,0:T(8,128)S(1)}, s32[192,384]{1,0:T(8,128)}, u32[]{:S(2)}) %copy-start.4) | copy-done | bytes 294936
  5.4 0.0 copy-start.5
  5.4 1.0 %copy-done.5 = f32[24,96,24]{1,2,0:T(8,128)S(1)} copy-done((f32[24,96,24]{1,2,0:T(8,128)S(1)}, f32[24,96,24]{1,2,0:T(8,128)}, u32[]{:S(2)}) %copy-start.5) | copy-done | bytes 221208
  6.4 41.0 %shard_map.93 = (f32[192,384]{1,0:T(8,128)S(1)}, f32[192,384]{1,0:T(8,128)S(1)}, f32[192,384]{1,0:T(8,128)S(1)}, f32[24,24]{1,0:T(8,128)S(1)}) custom-call(f32[192,384]{1,0:T(8,128)S(1)} %copy-done, f32[192,384]{1,0:T(8,128)S(1)} %copy-done.1, f32[192,384]{1,0:T(8,128)S(1)} %copy-done.2, f32[192,384]{1,0:T(8,128)S(1)} %copy-done.3, ...), custom_call_target="tpu_custom_call" | custom-call | tf_op jit(solution)/shard_map/pallas_call | solution.py:426
  47.4 0.7 %copy.14 = f32[192,384]{1,0:T(8,128)} copy(f32[192,384]{1,0:T(8,128)S(1)} %get-tuple-element.8) | data formatting | bytes 589824
  48.1 0.7 %copy.15 = f32[192,384]{1,0:T(8,128)} copy(f32[192,384]{1,0:T(8,128)S(1)} %get-tuple-element.9) | data formatting | bytes 589824
  48.8 0.7 %copy.16 = f32[192,384]{1,0:T(8,128)} copy(f32[192,384]{1,0:T(8,128)S(1)} %get-tuple-element.10) | data formatting | bytes 589824
  49.6 0.6 %copy.17 = f32[24,24]{1,0:T(8,128)} copy(f32[24,24]{1,0:T(8,128)S(1)} %get-tuple-element.11) | data formatting | bytes 4608
Async XLA Ops:
  0.6 1.0 %copy-start = (f32[192,384]{1,0:T(8,128)S(1)}, f32[192,384]{1,0:T(8,128)}, u32[]{:S(2)}) copy-start(f32[192,384]{1,0:T(8,128)} %height.1) | copy-start | bytes 884740
  1.6 1.0 %copy-start.1 = (f32[192,384]{1,0:T(8,128)S(1)}, f32[192,384]{1,0:T(8,128)}, u32[]{:S(2)}) copy-start(f32[192,384]{1,0:T(8,128)} %flux_lon.1) | copy-start | bytes 884740
  2.6 1.0 %copy-start.2 = (f32[192,384]{1,0:T(8,128)S(1)}, f32[192,384]{1,0:T(8,128)}, u32[]{:S(2)}) copy-start(f32[192,384]{1,0:T(8,128)} %flux_lat.1) | copy-start | bytes 884740
  3.5 1.0 %copy-start.3 = (f32[192,384]{1,0:T(8,128)S(1)}, f32[192,384]{1,0:T(8,128)}, u32[]{:S(2)}) copy-start(f32[192,384]{1,0:T(8,128)} %depth.1) | copy-start | bytes 884740
  4.5 1.0 %copy-start.4 = (s32[192,384]{1,0:T(8,128)S(1)}, s32[192,384]{1,0:T(8,128)}, u32[]{:S(2)}) copy-start(s32[192,384]{1,0:T(8,128)} %wet.1) | copy-start | bytes 884740
  5.4 1.0 %copy-start.5 = (f32[24,96,24]{1,2,0:T(8,128)S(1)}, f32[24,96,24]{1,2,0:T(8,128)}, u32[]{:S(2)}) copy-start(f32[24,96,24]{1,2,0:T(8,128)} %param.11) | copy-start | bytes 663556

commit v2 on v1

--- a/solution.py
+++ b/solution.py
@@ -64,7 +64,7 @@
     lat_n, lon_n,
     height, flux_lon, flux_lat, depth, wet, kernel,
     out_height, out_lon, out_lat, out_loading,
-    field, wet_in, kin, state, final, coef, rowc, zeta, gather_m, expand_m,
+    field, wet_in, kin, state, final, coef, rowc, ahead, gather_m, expand_m,
     kt, khi, klo, mslot, mass_all, psend, precv,
     lonh_send, lonh_recv, lath_send, lath_recv,
     in_sem, out_sem, mass_ss, mass_rs, all_ss, all_rs, part_ss, part_rs,
@@ -115,19 +115,12 @@
 
     cos_center = coslat(place + 0.5)
     rowc[0] = cos_center
-    rowc[1] = COURANT_LON / cos_center
-    rowc[2] = COURANT_LAT / cos_center * coslat(place + 1.0)
-    rowc[3] = COURANT_LAT / cos_center * coslat(place)
     row_ratio, col_ratio = rows // crows, cols // ccols
     gather_m[...] = jnp.where(
         lax.broadcasted_iota(jnp.int32, (cols, LANES), 0) // col_ratio == lane_of((cols, LANES)),
         1.0 / (row_ratio * col_ratio),
         0.0,
     ).astype(BF16)
-    fine = lane_of((LANES, all_cols))
-    fine = jnp.where(fine < cols + LANES // 2, 1 + fine // col_ratio, 0)
-    expand_m[...] = jnp.where(sub_of((LANES, all_cols)) == fine, 1.0, 0.0).astype(BF16)
-
     def wide(cells, count):
         return jnp.concatenate([cells] * count, 1)
 
@@ -232,32 +225,45 @@
             total = total + precv[step, off]
         return jnp.concatenate([turn(total, -32 * part, 1) for part in range(4)], 0)
 
-    def set_zeta(level, loading):
-        spread = exact_dot(loading, expand_m[...])
+    def prepare(level, old_lon, old_lat):
         sub = sub_of((SUB, all_cols))
-        for tile in range(tiles):
-            rise = jnp.broadcast_to(spread[tile : tile + 1], (SUB, all_cols))
+        for here in range(tiles):
+            at = pl.ds(here * SUB, SUB)
+            cells = level[at, :]
+            after = level[pl.ds((here + 1) % tiles * SUB, SUB), :]
+            rise_east = turn(cells, all_cols - 1, 1) - cells
+            rise_north = turn(jnp.where(sub == 0, after, cells), SUB - 1, 0) - cells
+            ahead[0, at, :] = coef[1, at, :] * old_lon[at, :] - coef[0, at, :] * rise_east
+            ahead[1, at, :] = coef[3, at, :] * old_lat[at, :] - coef[2, at, :] * rise_north
+
+    def spread(loading):
+        following = turn(loading, loading.shape[0] - 1, 0)
+        first = jnp.broadcast_to(loading[:1], loading.shape)
+        north_rise = jnp.where(sub_of(loading.shape) < crows, following - loading, first - following)
+        return exact_dot(loading, expand_m[1]), exact_dot(north_rise, expand_m[0])
+
+    def advance(level, loading, new, last):
+        sub = sub_of((SUB, all_cols))
+        east_rise, north_rise = spread(loading)
+        count = all_cols // LANES
+
+        def lat_of(tile):
+            at = pl.ds(tile * SUB, SUB)
+            rise = jnp.broadcast_to(north_rise[tile : tile + 1], (SUB, all_cols))
+            return ahead[1, at, :] - coef[2, at, :] * jnp.where(sub == SUB - 1, rise, 0.0)
+
+        below = lat_of(tiles - 1)
+        done = []
+        for tile in range(tiles - 1 if last else tiles):
+            at = pl.ds(tile * SUB, SUB)
+            rise = jnp.broadcast_to(east_rise[tile : tile + 1], (SUB, all_cols))
             if tile == tiles - 1:
-                below = jnp.broadcast_to(spread[tile + 1 : tile + 2], (SUB, all_cols))
-                rise = jnp.where(sub < SUB // 2, rise, below)
-            at = pl.ds(tile * SUB, SUB)
-            zeta[at, :] = level[at, :] + rise
-
-    def advance(level, old_lon, old_lat, new):
-        sub = sub_of((SUB, all_cols))
-
-        def one(turn_index, below):
-            here = lax.rem(turn_index + tiles - 1, tiles)
-            after = lax.rem(turn_index, tiles)
-            at = pl.ds(pl.multiple_of(here * SUB, SUB), SUB)
-            up_at = pl.ds(pl.multiple_of(after * SUB, SUB), SUB)
-            z = zeta[at, :]
-            z_north = turn(jnp.where(sub == 0, zeta[up_at, :], z), SUB - 1, 0)
-            z_east = turn(z, all_cols - 1, 1)
-            lon_new = coef[1, at, :] * old_lon[at, :] - coef[0, at, :] * (z_east - z)
-            lat_new = coef[3, at, :] * old_lat[at, :] - coef[2, at, :] * (z_north - z)
+                south_rise = jnp.broadcast_to(east_rise[tile + 1 : tile + 2], (SUB, all_cols))
+                rise = jnp.where(sub < SUB // 2, rise, south_rise)
+            lon_new = ahead[0, at, :] - coef[0, at, :] * rise
+            lat_new = lat_of(tile)
             lat_south = turn(jnp.where(sub == SUB - 1, below, lat_new), 1, 0)
-            count = all_cols // LANES
+            below = lat_new
             new[1, at, :] = lon_new
             new[2, at, :] = lat_new
             new[0, at, :] = field[4, at, :] * (
@@ -268,9 +274,18 @@
                     - wide(rowc[3, at, :], count) * lat_south
                 )
             )
-            return lat_new
-
-        lax.fori_loop(0, tiles + 1, one, jnp.zeros((SUB, all_cols), F32))
+            group = (tiles - 1) // 3
+            if last and tile % group == group - 1:
+                part = pl.ds((tile + 1 - group) * SUB, group * SUB)
+                for index, out in enumerate((out_height, out_lon, out_lat)):
+                    copy = pltpu.make_async_copy(
+                        new.at[index, part, pl.ds(0, cols)],
+                        out.at[part],
+                        out_sem.at[index, tile // group],
+                    )
+                    copy.start()
+                    done.append(copy)
+        return done
 
     loads[0].wait()
     loads[1].wait()
@@ -305,14 +320,9 @@
     pending += kh_copies
     kt[...] = jnp.zeros(kt.shape, F32)
 
-    band_copies = send_band(0, mass_copies)
-    pending += band_copies
-
     half = ccols // 2
-    for copy in kh_copies:
-        copy.wait_recv()
-
-    def one_row(row, carry):
+
+    def put(row):
         cells = kin[row]
         if jpad > jrows:
             cells = jnp.concatenate([cells, jnp.zeros((ccols, jpad - jrows), F32)], 1)
@@ -320,16 +330,22 @@
             for chunk in range(jpad // LANES):
                 piece = cells[part * half : (part + 1) * half, chunk * LANES : (chunk + 1) * LANES]
                 kt[part * (jpad // LANES) + chunk, pl.ds(row, half, stride=32), :] = piece
-        return carry
-
-    lax.fori_loop(0, crows + 2, one_row, 0)
+
+    for row in range(crows):
+        put(row)
+
+    band_copies = send_band(0, mass_copies)
+    pending += band_copies
+
+    for copy in kh_copies:
+        copy.wait_recv()
+    put(crows)
+    put(crows + 1)
     for chunk in range(kt.shape[0]):
         high, low = halves(kt[chunk])
         khi[:, chunk * LANES : (chunk + 1) * LANES] = high
         klo[:, chunk * LANES : (chunk + 1) * LANES] = low
 
-    part_copies = send_partials(0, band_copies)
-    pending += part_copies
 
     for copy in lonh_copies:
         copy.wait_recv()
@@ -355,6 +371,26 @@
         send(lath_send.at[1], lath_recv.at[1], lath_ss.at[1], lath_rs.at[1], (south, lon)),
     ]
     pending += lath_copies
+
+    cos_center = rowc[0]
+    rowc[1] = COURANT_LON / cos_center
+    rowc[2] = COURANT_LAT / cos_center * coslat(place + 1.0)
+    rowc[3] = COURANT_LAT / cos_center * coslat(place)
+    fine = lane_of((LANES, all_cols))
+
+    def coarse(column):
+        return jnp.where(column < cols + LANES // 2, 1 + column // col_ratio, 0)
+
+    own_cell = sub_of((LANES, all_cols)) == coarse(fine)
+    next_fine = jnp.where(fine == all_cols - 1, 0, fine + 1)
+    east_cell = sub_of((LANES, all_cols)) == coarse(next_fine)
+    own_cell, east_cell = jnp.where(own_cell, 1.0, 0.0), jnp.where(east_cell, 1.0, 0.0)
+    expand_m[0] = own_cell.astype(BF16)
+    expand_m[1] = (east_cell - own_cell).astype(BF16)
+
+    part_copies = send_partials(0, band_copies)
+    pending += part_copies
+
     for copy in lath_copies:
         copy.wait_recv()
     for index in range(5):
@@ -366,10 +402,9 @@
             from_north = jnp.where(lat == lat_n - 1, 0.0, 1.0) * from_north
         field[index, rows:, :] = jnp.where(sub < SUB // 2, from_north, from_south)
 
-    def factors(here, carry):
-        after = lax.rem(here + 1, tiles)
-        at = pl.ds(pl.multiple_of(here * SUB, SUB), SUB)
-        up_at = pl.ds(pl.multiple_of(after * SUB, SUB), SUB)
+    for here in range(tiles):
+        at = pl.ds(here * SUB, SUB)
+        up_at = pl.ds((here + 1) % tiles * SUB, SUB)
         deep, sea = field[3, at, :], field[4, at, :]
         deep_north = turn(jnp.where(sub == 0, field[3, up_at, :], deep), SUB - 1, 0)
         sea_north = turn(jnp.where(sub == 0, field[4, up_at, :], sea), SUB - 1, 0)
@@ -383,27 +418,18 @@
         both = sea * sea_north
         coef[3, at, :] = both
         coef[2, at, :] = both * (COURANT_LAT * 0.5) * (deep + deep_north)
-        return carry
-
-    lax.fori_loop(0, tiles, factors, 0)
-
-    set_zeta(field.at[0], loading_of(0, part_copies))
-    advance(field.at[0], field.at[1], field.at[2], state)
+    prepare(field.at[0], field.at[1], field.at[2])
+
+    advance(field.at[0], loading_of(0, part_copies), state, False)
 
     mass_copies = send_mass(1, state[0, :rows, :cols])
+    prepare(state.at[0], state.at[1], state.at[2])
     band_copies = send_band(1, mass_copies)
     part_copies = send_partials(1, band_copies)
     pending += mass_copies + band_copies + part_copies
     loading = loading_of(1, part_copies)
-    set_zeta(state.at[0], loading)
-    advance(state.at[0], state.at[1], state.at[2], final)
-    results = [
-        pltpu.make_async_copy(final.at[(index, *own)], out, out_sem.at[index])
-        for index, out in enumerate((out_height, out_lon, out_lat))
-    ]
-    for copy in results:
-        copy.start()
     out_loading[...] = turn(loading[:crows], -1, 1)[:, :ccols]
+    results = advance(state.at[0], loading, final, True)
     for copy in pending:
         copy.wait_send()
     for copy in results:
@@ -436,9 +462,9 @@
             pltpu.VMEM((3, all_rows, all_cols), F32),
             pltpu.VMEM((4, all_rows, all_cols), F32),
             pltpu.VMEM((4, all_rows, LANES), F32),
-            pltpu.VMEM((all_rows, all_cols), F32),
+            pltpu.VMEM((2, all_rows, all_cols), F32),
             pltpu.VMEM((cols, LANES), BF16),
-            pltpu.VMEM((LANES, all_cols), BF16),
+            pltpu.VMEM((2, LANES, all_cols), BF16),
             pltpu.VMEM((2 * jpad // LANES, lags, LANES), F32),
             pltpu.VMEM((lags, 2 * jpad), BF16),
             pltpu.VMEM((lags, 2 * jpad), BF16),
@@ -451,7 +477,7 @@
             pltpu.VMEM((2, 16, all_cols), F32),
             pltpu.VMEM((2, 16, all_cols), F32),
             dma((6,)),
-            dma((3,)),
+            dma((3, 3)),
             dma((STEPS, lon_n)),
             dma((STEPS, lon_n)),
             dma((STEPS, lat_n)),
@@ -466,7 +492,7 @@
             dma((2,)),
         ],
         compiler_params=pltpu.CompilerParams(
-            collective_id=0, has_side_effects=True, vmem_limit_bytes=40 * 2**20
+            collective_id=0, has_side_effects=True, vmem_limit_bytes=64 * 2**20
         ),
     )(height, flux_lon, flux_lat, depth, wet, kernel)
 

time: 50.5 us -> 37.7 us (0.75)
  Pallas kernels: 41 us -> 32.7 us
  local copies, waits for them, and re-layouts: 8.5 us -> 4.13 us
    pallas_call x1, Pallas kernels: 41 us -> 32.7 us  [body(): pl.pallas_call(functools.partial(run, lat_n, lon_n), out_shape=[block, bl...]
    unnamed x16 -> x10, local copies, waits for them, and re-layouts: 8.5 us -> 4.13 us
where the time goes in v2:
time: 37.7 us; the launch traced here: 37.5 us
  Pallas kernels  32.7 us (87%)
  local copies, waits for them, and re-layouts  4.13 us (11%)
  between operations  0.65 us (2%)
    pallas_call x1, Pallas kernels, body(): pl.pallas_call(functools.partial(run, lat_n, lon_n), out_shape=[block, bl...  32.7 us
    unnamed x10, local copies, waits for them, and re-layouts  4.13 us

profile of v2, /device:TPU:0, one launch (start us, length us, event | category | flops | bytes accessed | tf_op | source)
XLA Modules:
  0.0 37.5 jit_solution(4353033055923555820)
XLA Ops:
  0.6 32.7 %shard_map.93 = (f32[192,384]{1,0:T(8,128)}, f32[192,384]{1,0:T(8,128)}, f32[192,384]{1,0:T(8,128)}, f32[24,24]{1,0:T(8,128)}) custom-call(f32[192,384]{1,0:T(8,128)} %height.1, f32[192,384]{1,0:T(8,128)} %flux_lon.1, f32[192,384]{1,0:T(8,128)} %flux_lat.1, f32[192,384]{1,0:T(8,128)} %depth.1, s32[192,384]{1,0:T(8,128)} %wet.1, f32[24,24,96]{2,1,0:T(8,128)} %bitcast.1), custom_call_target="tpu_custom_call" | custom-call | tf_op jit(solution)/shard_map/pallas_call | solution.py:452
  33.3 0.0 copy-start.1
  33.4 1.7 %copy.14 = f32[192,384]{1,0:T(8,128)} copy(f32[192,384]{1,0:T(8,128)} %get-tuple-element.8) | data formatting | bytes 589824
  35.1 0.0 copy-done.1
  35.1 0.0 copy-start
  35.1 0.7 %copy.15 = f32[192,384]{1,0:T(8,128)} copy(f32[192,384]{1,0:T(8,128)S(1)} %copy-done.1) | data formatting | bytes 589824
  35.8 0.4 copy-done
  36.2 0.0 copy-start.2
  36.2 0.7 %copy.16 = f32[192,384]{1,0:T(8,128)} copy(f32[192,384]{1,0:T(8,128)S(1)} %copy-done) | data formatting | bytes 589824
  36.9 0.0 copy-done.2
  36.9 0.6 %copy.17 = f32[24,24]{1,0:T(8,128)} copy(f32[24,24]{1,0:T(8,128)S(1)} %copy-done.2) | data formatting | bytes 4608
Async XLA Ops:
  33.3 1.8 %copy-start.1 = (f32[192,384]{1,0:T(8,128)S(1)}, f32[192,384]{1,0:T(8,128)}, u32[]{:S(2)}) copy-start(f32[192,384]{1,0:T(8,128)} %get-tuple-element.9) | copy-start | bytes 884740
  35.1 1.1 %copy-start = (f32[192,384]{1,0:T(8,128)S(1)}, f32[192,384]{1,0:T(8,128)}, u32[]{:S(2)}) copy-start(f32[192,384]{1,0:T(8,128)} %get-tuple-element.10) | copy-start | bytes 884740
  36.2 0.7 %copy-start.2 = (f32[24,24]{1,0:T(8,128)S(1)}, f32[24,24]{1,0:T(8,128)}, u32[]{:S(2)}) copy-start(f32[24,24]{1,0:T(8,128)} %get-tuple-element.11) | copy-start | bytes 6916

commit v3 on v2

--- a/solution.py
+++ b/solution.py
@@ -121,6 +121,21 @@
         1.0 / (row_ratio * col_ratio),
         0.0,
     ).astype(BF16)
+    rowc[1] = COURANT_LON / cos_center
+    rowc[2] = COURANT_LAT / cos_center * coslat(place + 1.0)
+    rowc[3] = COURANT_LAT / cos_center * coslat(place)
+    fine = lane_of((LANES, all_cols))
+
+    def coarse(column):
+        return jnp.where(column < cols + LANES // 2, 1 + column // col_ratio, 0)
+
+    own_cell = sub_of((LANES, all_cols)) == coarse(fine)
+    next_fine = jnp.where(fine == all_cols - 1, 0, fine + 1)
+    east_cell = sub_of((LANES, all_cols)) == coarse(next_fine)
+    own_cell, east_cell = jnp.where(own_cell, 1.0, 0.0), jnp.where(east_cell, 1.0, 0.0)
+    expand_m[0] = own_cell.astype(BF16)
+    expand_m[1] = (east_cell - own_cell).astype(BF16)
+
     def wide(cells, count):
         return jnp.concatenate([cells] * count, 1)
 
@@ -372,22 +387,6 @@
     ]
     pending += lath_copies
 
-    cos_center = rowc[0]
-    rowc[1] = COURANT_LON / cos_center
-    rowc[2] = COURANT_LAT / cos_center * coslat(place + 1.0)
-    rowc[3] = COURANT_LAT / cos_center * coslat(place)
-    fine = lane_of((LANES, all_cols))
-
-    def coarse(column):
-        return jnp.where(column < cols + LANES // 2, 1 + column // col_ratio, 0)
-
-    own_cell = sub_of((LANES, all_cols)) == coarse(fine)
-    next_fine = jnp.where(fine == all_cols - 1, 0, fine + 1)
-    east_cell = sub_of((LANES, all_cols)) == coarse(next_fine)
-    own_cell, east_cell = jnp.where(own_cell, 1.0, 0.0), jnp.where(east_cell, 1.0, 0.0)
-    expand_m[0] = own_cell.astype(BF16)
-    expand_m[1] = (east_cell - own_cell).astype(BF16)
-
     part_copies = send_partials(0, band_copies)
     pending += part_copies
 
@@ -436,6 +435,19 @@
         copy.wait()
 
 
+def hand_over(*refs):
+    sems = refs[-1]
+    count = len(refs) // 2
+    copies = [
+        pltpu.make_async_copy(refs[index], refs[count + index], sems.at[index])
+        for index in range(count)
+    ]
+    for copy in copies:
+        copy.start()
+    for copy in copies:
+        copy.wait()
+
+
 def body(height, flux_lon, flux_lat, depth, wet, kernel):
     lat_n, lon_n = lax.axis_size("lat"), lax.axis_size("lon")
     rows, cols = height.shape
@@ -449,7 +461,7 @@
     dma = pltpu.SemaphoreType.DMA
     block = jax.ShapeDtypeStruct((rows, cols), F32)
     anywhere = pl.BlockSpec(memory_space=pl.ANY)
-    return pl.pallas_call(
+    results = pl.pallas_call(
         functools.partial(run, lat_n, lon_n),
         out_shape=[block, block, block, jax.ShapeDtypeStruct((crows, ccols), F32)],
         in_specs=[anywhere] * 6,
@@ -495,6 +507,14 @@
             collective_id=0, has_side_effects=True, vmem_limit_bytes=64 * 2**20
         ),
     )(height, flux_lon, flux_lat, depth, wet, kernel)
+    return pl.pallas_call(
+        hand_over,
+        out_shape=[jax.ShapeDtypeStruct(result.shape, F32) for result in results],
+        in_specs=[anywhere] * 4,
+        out_specs=[anywhere] * 4,
+        scratch_shapes=[dma((4,))],
+        compiler_params=pltpu.CompilerParams(vmem_limit_bytes=64 * 2**20),
+    )(*results)
 
 
 def solution(mesh):

time: 37.7 us -> 61.8 us (1.64)
  Pallas kernels: 32.7 us -> 61.1 us
  local copies, waits for them, and re-layouts: 4.13 us -> 0 us
    pallas_call x0 -> x1, Pallas kernels: none -> 28.3 us  [body(): pl.pallas_call(hand_over, out_shape=[jax.ShapeDtypeStruct(result.shape, F...]
    unnamed x10 -> x0, local copies, waits for them, and re-layouts: 4.13 us -> none
where the time goes in v3:
time: 61.8 us; the launch traced here: 61.7 us
  Pallas kernels  61.1 us (99%)
  between operations  0.64 us (1%)
    pallas_call x1, Pallas kernels, body(): pl.pallas_call(functools.partial(run, lat_n, lon_n), out_shape=[block, bl...  32.7 us
    pallas_call x1, Pallas kernels, body(): pl.pallas_call(hand_over, out_shape=[jax.ShapeDtypeStruct(result.shape, F...  28.3 us

profile of v3, /device:TPU:0, one launch (start us, length us, event | category | flops | bytes accessed | tf_op | source)
XLA Modules:
  0.0 61.7 jit_solution(6126979667369135003)
XLA Ops:
  0.6 32.7 %shard_map.93 = (f32[192,384]{1,0:T(8,128)}, f32[192,384]{1,0:T(8,128)}, f32[192,384]{1,0:T(8,128)}, f32[24,24]{1,0:T(8,128)}) custom-call(f32[192,384]{1,0:T(8,128)} %height.1, f32[192,384]{1,0:T(8,128)} %flux_lon.1, f32[192,384]{1,0:T(8,128)} %flux_lat.1, f32[192,384]{1,0:T(8,128)} %depth.1, s32[192,384]{1,0:T(8,128)} %wet.1, f32[24,24,96]{2,1,0:T(8,128)} %bitcast.1), custom_call_target="tpu_custom_call" | custom-call | tf_op jit(solution)/shard_map/pallas_call | solution.py:464
  33.4 28.3 %shard_map.94 = (f32[192,384]{1,0:T(8,128)}, f32[192,384]{1,0:T(8,128)}, f32[192,384]{1,0:T(8,128)}, f32[24,24]{1,0:T(8,128)}) custom-call(f32[192,384]{1,0:T(8,128)} %get-tuple-element.8.refs_0_, f32[192,384]{1,0:T(8,128)} %get-tuple-element.9.refs_1_, f32[192,384]{1,0:T(8,128)} %get-tuple-element.10.refs_2_, f32[24,24]{1,0:T(8,128)} %get-tuple-element.11.refs_3_), custom_call_target="tpu_custom_call" | custom-call | tf_op jit(solution)/shard_map/pallas_call | solution.py:510

commit v4 on v2

--- a/solution.py
+++ b/solution.py
@@ -60,11 +60,129 @@
     return summed[:rows] + (summed[rows : 2 * rows] + summed[2 * rows :])
 
 
+def wide(cells, count):
+    return jnp.concatenate([cells] * count, 1)
+
+
+def expanders(all_cols, cols, col_ratio):
+    shape = (LANES, all_cols)
+    fine = lane_of(shape)
+
+    def cell(column):
+        coarse = jnp.where(column < cols + LANES // 2, 1 + column // col_ratio, 0)
+        return jnp.where(sub_of(shape) == coarse, 1.0, 0.0)
+
+    own = cell(fine)
+    east = cell(jnp.where(fine == all_cols - 1, 0, fine + 1))
+    return own.astype(BF16), (east - own).astype(BF16)
+
+
+def spread(loading, crows, expand, expand_rise):
+    following = turn(loading, loading.shape[0] - 1, 0)
+    first = jnp.broadcast_to(loading[:1], loading.shape)
+    north_rise = jnp.where(sub_of(loading.shape) < crows, following - loading, first - following)
+    return exact_dot(loading, expand_rise), exact_dot(north_rise, expand)
+
+
+def advance(level, ahead, factor, sea, rowc, rises, new, last, before, after):
+    all_rows, all_cols = level.shape
+    tiles = all_rows // SUB
+    sub = sub_of((SUB, all_cols))
+    east_rise, north_rise = rises
+    count = all_cols // LANES
+
+    def lat_of(tile):
+        at = pl.ds(tile * SUB, SUB)
+        rise = jnp.broadcast_to(north_rise[tile : tile + 1], (SUB, all_cols))
+        return ahead[1][at, :] - factor[1][at, :] * jnp.where(sub == SUB - 1, rise, 0.0)
+
+    before(tiles - 1)
+    below = lat_of(tiles - 1)
+    for tile in range(tiles - 1 if last else tiles):
+        before(tile)
+        at = pl.ds(tile * SUB, SUB)
+        rise = jnp.broadcast_to(east_rise[tile : tile + 1], (SUB, all_cols))
+        if tile == tiles - 1:
+            south_rise = jnp.broadcast_to(east_rise[tile + 1 : tile + 2], (SUB, all_cols))
+            rise = jnp.where(sub < SUB // 2, rise, south_rise)
+        lon_new = ahead[0][at, :] - factor[0][at, :] * rise
+        lat_new = lat_of(tile)
+        lat_south = turn(jnp.where(sub == SUB - 1, below, lat_new), 1, 0)
+        below = lat_new
+        new[1, at, :] = lon_new
+        new[2, at, :] = lat_new
+        new[0, at, :] = sea[at, :] * (
+            level[at, :]
+            - wide(rowc[1, at, :], count) * (lon_new - turn(lon_new, 1, 1))
+            - (
+                wide(rowc[2, at, :], count) * lat_new
+                - wide(rowc[3, at, :], count) * lat_south
+            )
+        )
+        after(tile)
+
+
+GROUPS = 3
+
+
+def finish(
+    pack, rowc_in, loading_in, out_height, out_lon, out_lat, out_loading,
+    have, rowc, loading_ref, final, pack_sem, row_sem, load_sem, out_sem,
+):
+    rows, cols = out_height.shape
+    crows, ccols = out_loading.shape
+    all_rows, all_cols = have.shape[1:]
+    tiles = all_rows // SUB
+    group = rows // GROUPS
+    get_loading = pltpu.make_async_copy(loading_in, loading_ref, load_sem)
+    get_rowc = pltpu.make_async_copy(rowc_in, rowc, row_sem)
+    parts = [pl.ds(rows, SUB)] + [pl.ds(index * group, group) for index in range(GROUPS)]
+    gets = [
+        pltpu.make_async_copy(pack.at[:, part], have.at[:, part], pack_sem.at[index])
+        for index, part in enumerate(parts)
+    ]
+    for copy in [get_loading, get_rowc, *gets]:
+        copy.start()
+    expand, expand_rise = expanders(all_cols, cols, cols // ccols)
+    get_loading.wait()
+    loading = loading_ref[...]
+    out_loading[...] = turn(loading[:crows], -1, 1)[:, :ccols]
+    rises = spread(loading, crows, expand, expand_rise)
+    get_rowc.wait()
+    puts = []
+    per = group // SUB
+
+    def before(tile):
+        if tile == tiles - 1:
+            gets[0].wait()
+        elif tile % per == 0:
+            gets[1 + tile // per].wait()
+
+    def after(tile):
+        if tile % per == per - 1:
+            part = parts[1 + tile // per]
+            for index, out in enumerate((out_height, out_lon, out_lat)):
+                copy = pltpu.make_async_copy(
+                    final.at[index, part, pl.ds(0, cols)],
+                    out.at[part],
+                    out_sem.at[index, tile // per],
+                )
+                copy.start()
+                puts.append(copy)
+
+    advance(
+        have.at[5], (have.at[3], have.at[4]), (have.at[0], have.at[1]), have.at[2], rowc, rises,
+        final, True, before, after,
+    )
+    for copy in puts:
+        copy.wait()
+
+
 def run(
     lat_n, lon_n,
     height, flux_lon, flux_lat, depth, wet, kernel,
-    out_height, out_lon, out_lat, out_loading,
-    field, wet_in, kin, state, final, coef, rowc, ahead, gather_m, expand_m,
+    out_pack, out_rowc, out_loading,
+    field, wet_in, kin, state, coef, rowc, ahead, gather_m, expand_m,
     kt, khi, klo, mslot, mass_all, psend, precv,
     lonh_send, lonh_recv, lath_send, lath_recv,
     in_sem, out_sem, mass_ss, mass_rs, all_ss, all_rs, part_ss, part_rs,
@@ -121,8 +239,10 @@
         1.0 / (row_ratio * col_ratio),
         0.0,
     ).astype(BF16)
-    def wide(cells, count):
-        return jnp.concatenate([cells] * count, 1)
+    rowc[1] = COURANT_LON / cos_center
+    rowc[2] = COURANT_LAT / cos_center * coslat(place + 1.0)
+    rowc[3] = COURANT_LAT / cos_center * coslat(place)
+    expand_m[0], expand_m[1] = expanders(all_cols, cols, col_ratio)
 
     def send_mass(step, level):
         weighted = level * field[4, :rows, :cols] * wide(rowc[0, :rows], cols // LANES)
@@ -225,7 +345,7 @@
             total = total + precv[step, off]
         return jnp.concatenate([turn(total, -32 * part, 1) for part in range(4)], 0)
 
-    def prepare(level, old_lon, old_lat):
+    def prepare(step, level, old_lon, old_lat):
         sub = sub_of((SUB, all_cols))
         for here in range(tiles):
             at = pl.ds(here * SUB, SUB)
@@ -233,59 +353,8 @@
             after = level[pl.ds((here + 1) % tiles * SUB, SUB), :]
             rise_east = turn(cells, all_cols - 1, 1) - cells
             rise_north = turn(jnp.where(sub == 0, after, cells), SUB - 1, 0) - cells
-            ahead[0, at, :] = coef[1, at, :] * old_lon[at, :] - coef[0, at, :] * rise_east
-            ahead[1, at, :] = coef[3, at, :] * old_lat[at, :] - coef[2, at, :] * rise_north
-
-    def spread(loading):
-        following = turn(loading, loading.shape[0] - 1, 0)
-        first = jnp.broadcast_to(loading[:1], loading.shape)
-        north_rise = jnp.where(sub_of(loading.shape) < crows, following - loading, first - following)
-        return exact_dot(loading, expand_m[1]), exact_dot(north_rise, expand_m[0])
-
-    def advance(level, loading, new, last):
-        sub = sub_of((SUB, all_cols))
-        east_rise, north_rise = spread(loading)
-        count = all_cols // LANES
-
-        def lat_of(tile):
-            at = pl.ds(tile * SUB, SUB)
-            rise = jnp.broadcast_to(north_rise[tile : tile + 1], (SUB, all_cols))
-            return ahead[1, at, :] - coef[2, at, :] * jnp.where(sub == SUB - 1, rise, 0.0)
-
-        below = lat_of(tiles - 1)
-        done = []
-        for tile in range(tiles - 1 if last else tiles):
-            at = pl.ds(tile * SUB, SUB)
-            rise = jnp.broadcast_to(east_rise[tile : tile + 1], (SUB, all_cols))
-            if tile == tiles - 1:
-                south_rise = jnp.broadcast_to(east_rise[tile + 1 : tile + 2], (SUB, all_cols))
-                rise = jnp.where(sub < SUB // 2, rise, south_rise)
-            lon_new = ahead[0, at, :] - coef[0, at, :] * rise
-            lat_new = lat_of(tile)
-            lat_south = turn(jnp.where(sub == SUB - 1, below, lat_new), 1, 0)
-            below = lat_new
-            new[1, at, :] = lon_new
-            new[2, at, :] = lat_new
-            new[0, at, :] = field[4, at, :] * (
-                level[at, :]
-                - wide(rowc[1, at, :], count) * (lon_new - turn(lon_new, 1, 1))
-                - (
-                    wide(rowc[2, at, :], count) * lat_new
-                    - wide(rowc[3, at, :], count) * lat_south
-                )
-            )
-            group = (tiles - 1) // 3
-            if last and tile % group == group - 1:
-                part = pl.ds((tile + 1 - group) * SUB, group * SUB)
-                for index, out in enumerate((out_height, out_lon, out_lat)):
-                    copy = pltpu.make_async_copy(
-                        new.at[index, part, pl.ds(0, cols)],
-                        out.at[part],
-                        out_sem.at[index, tile // group],
-                    )
-                    copy.start()
-                    done.append(copy)
-        return done
+            ahead[step, 0, at, :] = coef[1, at, :] * old_lon[at, :] - coef[0, at, :] * rise_east
+            ahead[step, 1, at, :] = coef[3, at, :] * old_lat[at, :] - coef[2, at, :] * rise_north
 
     loads[0].wait()
     loads[1].wait()
@@ -372,22 +441,6 @@
     ]
     pending += lath_copies
 
-    cos_center = rowc[0]
-    rowc[1] = COURANT_LON / cos_center
-    rowc[2] = COURANT_LAT / cos_center * coslat(place + 1.0)
-    rowc[3] = COURANT_LAT / cos_center * coslat(place)
-    fine = lane_of((LANES, all_cols))
-
-    def coarse(column):
-        return jnp.where(column < cols + LANES // 2, 1 + column // col_ratio, 0)
-
-    own_cell = sub_of((LANES, all_cols)) == coarse(fine)
-    next_fine = jnp.where(fine == all_cols - 1, 0, fine + 1)
-    east_cell = sub_of((LANES, all_cols)) == coarse(next_fine)
-    own_cell, east_cell = jnp.where(own_cell, 1.0, 0.0), jnp.where(east_cell, 1.0, 0.0)
-    expand_m[0] = own_cell.astype(BF16)
-    expand_m[1] = (east_cell - own_cell).astype(BF16)
-
     part_copies = send_partials(0, band_copies)
     pending += part_copies
 
@@ -418,18 +471,39 @@
         both = sea * sea_north
         coef[3, at, :] = both
         coef[2, at, :] = both * (COURANT_LAT * 0.5) * (deep + deep_north)
-    prepare(field.at[0], field.at[1], field.at[2])
-
-    advance(field.at[0], loading_of(0, part_copies), state, False)
+    prepare(0, field.at[0], field.at[1], field.at[2])
+
+    results = []
+
+    def keep(*pairs):
+        for src, dst in pairs:
+            copy = pltpu.make_async_copy(src, dst, out_sem.at[len(results)])
+            copy.start()
+            results.append(copy)
+
+    keep(
+        (rowc, out_rowc),
+        (coef.at[0], out_pack.at[0]),
+        (coef.at[2], out_pack.at[1]),
+        (field.at[4], out_pack.at[2]),
+    )
+    rises = spread(loading_of(0, part_copies), crows, expand_m[0], expand_m[1])
+    advance(
+        field.at[0], (ahead.at[0, 0], ahead.at[0, 1]), (coef.at[0], coef.at[2]), field.at[4],
+        rowc, rises, state, False, lambda tile: None, lambda tile: None,
+    )
 
     mass_copies = send_mass(1, state[0, :rows, :cols])
-    prepare(state.at[0], state.at[1], state.at[2])
+    prepare(1, state.at[0], state.at[1], state.at[2])
+    keep(
+        (ahead.at[1, 0], out_pack.at[3]),
+        (ahead.at[1, 1], out_pack.at[4]),
+        (state.at[0], out_pack.at[5]),
+    )
     band_copies = send_band(1, mass_copies)
     part_copies = send_partials(1, band_copies)
     pending += mass_copies + band_copies + part_copies
-    loading = loading_of(1, part_copies)
-    out_loading[...] = turn(loading[:crows], -1, 1)[:, :ccols]
-    results = advance(state.at[0], loading, final, True)
+    out_loading[...] = loading_of(1, part_copies)
     for copy in pending:
         copy.wait_send()
     for copy in results:
@@ -448,21 +522,23 @@
     lags = 32 * ccols // 2
     dma = pltpu.SemaphoreType.DMA
     block = jax.ShapeDtypeStruct((rows, cols), F32)
+    inside = pl.BlockSpec(memory_space=pltpu.VMEM)
+    pack = jax.ShapeDtypeStruct((6, all_rows, all_cols), F32)
+    factors = jax.ShapeDtypeStruct((4, all_rows, LANES), F32)
     anywhere = pl.BlockSpec(memory_space=pl.ANY)
-    return pl.pallas_call(
+    results = pl.pallas_call(
         functools.partial(run, lat_n, lon_n),
-        out_shape=[block, block, block, jax.ShapeDtypeStruct((crows, ccols), F32)],
+        out_shape=[pack, factors, jax.ShapeDtypeStruct((32, LANES), F32)],
         in_specs=[anywhere] * 6,
-        out_specs=[anywhere] * 3 + [pl.BlockSpec(memory_space=pltpu.VMEM)],
+        out_specs=[anywhere, anywhere, inside],
         scratch_shapes=[
             pltpu.VMEM((5, all_rows, all_cols), F32),
             pltpu.VMEM((rows, cols), jnp.int32),
             pltpu.VMEM((crows + 2, ccols, jrows), F32),
             pltpu.VMEM((3, all_rows, all_cols), F32),
-            pltpu.VMEM((3, all_rows, all_cols), F32),
             pltpu.VMEM((4, all_rows, all_cols), F32),
             pltpu.VMEM((4, all_rows, LANES), F32),
-            pltpu.VMEM((2, all_rows, all_cols), F32),
+            pltpu.VMEM((STEPS, 2, all_rows, all_cols), F32),
             pltpu.VMEM((cols, LANES), BF16),
             pltpu.VMEM((2, LANES, all_cols), BF16),
             pltpu.VMEM((2 * jpad // LANES, lags, LANES), F32),
@@ -477,7 +553,7 @@
             pltpu.VMEM((2, 16, all_cols), F32),
             pltpu.VMEM((2, 16, all_cols), F32),
             dma((6,)),
-            dma((3, 3)),
+            dma((7,)),
             dma((STEPS, lon_n)),
             dma((STEPS, lon_n)),
             dma((STEPS, lat_n)),
@@ -495,6 +571,23 @@
             collective_id=0, has_side_effects=True, vmem_limit_bytes=64 * 2**20
         ),
     )(height, flux_lon, flux_lat, depth, wet, kernel)
+    return pl.pallas_call(
+        finish,
+        out_shape=[block, block, block, jax.ShapeDtypeStruct((crows, ccols), F32)],
+        in_specs=[anywhere] * 3,
+        out_specs=[anywhere] * 3 + [inside],
+        scratch_shapes=[
+            pltpu.VMEM((6, all_rows, all_cols), F32),
+            pltpu.VMEM((4, all_rows, LANES), F32),
+            pltpu.VMEM((32, LANES), F32),
+            pltpu.VMEM((3, all_rows, all_cols), F32),
+            dma((GROUPS + 1,)),
+            dma(()),
+            dma(()),
+            dma((3, GROUPS)),
+        ],
+        compiler_params=pltpu.CompilerParams(vmem_limit_bytes=64 * 2**20),
+    )(*results)
 
 
 def solution(mesh):

time: 37.7 us -> 35.5 us (0.942)
  local copies, waits for them, and re-layouts: 4.13 us -> 0 us
  Pallas kernels: 32.7 us -> 34.7 us
    unnamed x10 -> x0, local copies, waits for them, and re-layouts: 4.13 us -> none
    pallas_call x1 -> x2, Pallas kernels: 32.7 us -> 34.7 us  [the longest x1 31.3 us: body(): pl.pallas_call(functools.partial(run, lat_n, lon_n), out_shape=[pack, fac...]
where the time goes in v4:
time: 35.5 us; the launch traced here: 35.3 us
  Pallas kernels  34.7 us (98%)
  between operations  0.64 us (2%)
    pallas_call x1, Pallas kernels, body(): pl.pallas_call(functools.partial(run, lat_n, lon_n), out_shape=[pack, fac...  31.3 us
    pallas_call x1, Pallas kernels, body(): pl.pallas_call(finish, out_shape=[block, block, block, jax.ShapeDtypeStru...  3.36 us

profile of v4, /device:TPU:0, one launch (start us, length us, event | category | flops | bytes accessed | tf_op | source)
XLA Modules:
  0.0 35.3 jit_solution(5186457616463048847)
XLA Ops:
  0.6 31.3 %shard_map.93 = (f32[6,200,512]{2,1,0:T(8,128)}, f32[4,200,128]{2,1,0:T(8,128)}, f32[32,128]{1,0:T(8,128)}) custom-call(f32[192,384]{1,0:T(8,128)} %height.1, f32[192,384]{1,0:T(8,128)} %flux_lon.1, f32[192,384]{1,0:T(8,128)} %flux_lat.1, f32[192,384]{1,0:T(8,128)} %depth.1, s32[192,384]{1,0:T(8,128)} %wet.1, f32[24,24,96]{2,1,0:T(8,128)} %bitcast.1), custom_call_target="tpu_custom_call" | custom-call | tf_op jit(solution)/shard_map/pallas_call | solution.py:529
  32.0 3.4 %shard_map.94 = (f32[192,384]{1,0:T(8,128)}, f32[192,384]{1,0:T(8,128)}, f32[192,384]{1,0:T(8,128)}, f32[24,24]{1,0:T(8,128)}) custom-call(f32[6,200,512]{2,1,0:T(8,128)} %get-tuple-element.7.pack, f32[4,200,128]{2,1,0:T(8,128)} %get-tuple-element.8.rowc_in, f32[32,128]{1,0:T(8,128)} %get-tuple-element.9.loading_in), custom_call_target="tpu_custom_call" | custom-call | tf_op jit(solution)/shard_map/pallas_call | solution.py:574

commit v5 on v4

--- a/solution.py
+++ b/solution.py
@@ -183,7 +183,7 @@
     height, flux_lon, flux_lat, depth, wet, kernel,
     out_pack, out_rowc, out_loading,
     field, wet_in, kin, state, coef, rowc, ahead, gather_m, expand_m,
-    kt, khi, klo, mslot, mass_all, psend, precv,
+    kt, khi, klo, mslot, psend, precv,
     lonh_send, lonh_recv, lath_send, lath_recv,
     in_sem, out_sem, mass_ss, mass_rs, all_ss, all_rs, part_ss, part_rs,
     kh_ss, kh_rs, lonh_ss, lonh_rs, lath_ss, lath_rs,
@@ -194,7 +194,7 @@
     all_rows, all_cols = field.shape[1:]
     tiles = all_rows // SUB
     jpad = up(jrows, LANES)
-    width = mass_all.shape[2]
+    width = up(ccols * lon_n + ccols + 1, LANES)
     north, south = lax.rem(lat + 1, lat_n), lax.rem(lat + lat_n - 1, lat_n)
     east, west = lax.rem(lon + 1, lon_n), lax.rem(lon + lon_n - 1, lon_n)
     lon_peer = [lax.rem(lon + off, lon_n) for off in range(lon_n)]
@@ -253,47 +253,60 @@
         for part in range(1, crows // SUB):
             moved = turn(mass[part * SUB : (part + 1) * SUB], 32 * part, 1)
             packed = jnp.where(lanes >= 32 * part, moved, packed)
-        mslot[step, lon] = packed
+        mslot[step, lat, lon] = packed
         if step == 0:
             pl.semaphore_wait(barrier, lon_n + lat_n - 2)
+        lon_copies = []
+        for off in sorted(range(1, lon_n), key=lambda off: -min(off, lon_n - off)):
+            lon_copies.append(
+                (
+                    off,
+                    send(
+                        mslot.at[step, lat, lon], mslot.at[step, lat, lon],
+                        mass_ss.at[step, off], mass_rs.at[step, off], (lat, lon_peer[off]),
+                    ),
+                )
+            )
+        return lon_copies, forward(step, 0)
+
+    def forward(step, lon_off):
+        slot = lax.rem(lon + lon_n - lon_off, lon_n)
         return [
             send(
-                mslot.at[step, lon], mslot.at[step, lon],
-                mass_ss.at[step, off], mass_rs.at[step, off], (lat, lon_peer[off]),
+                mslot.at[step, lat, slot], mslot.at[step, lat, slot],
+                all_ss.at[step, off, lon_off], all_rs.at[step, off, lon_off],
+                (lat_peer[off], lon),
             )
-            for off in range(1, lon_n)
+            for off in range(1, lat_n)
         ]
 
-    def send_band(step, copies):
-        for copy in copies:
+    def send_band(step, lon_copies):
+        copies = []
+        for lon_off, copy in reversed(lon_copies):
             copy.wait_recv()
+            copies += forward(step, lon_off)
+        return copies
+
+    def band_of(step, band):
         lanes = lane_of((SUB, LANES))
-        bands = []
+        rows_of = []
         for part in range(crows // SUB):
             pieces = [jnp.zeros((SUB, LANES), F32) for _ in range(width // LANES)]
             for block in range(-(-width // ccols)):
                 first = ccols * block
-                slot = mslot[step, (block - 1) % lon_n]
+                slot = mslot[step, band, (block - 1) % lon_n]
                 moved = turn(slot, first - 32 * part, 1)
                 low, begin = first // LANES, first % LANES
                 pieces[low] = jnp.where(lanes >= begin, moved, pieces[low])
                 if begin + ccols > LANES and low + 1 < width // LANES:
                     pieces[low + 1] = moved
-            bands.append(jnp.concatenate(pieces, 1))
-        here = pl.ds(pl.multiple_of(lat * crows, SUB), crows)
-        mass_all[step, here] = jnp.concatenate(bands, 0)
-        return [
-            send(
-                mass_all.at[step, here], mass_all.at[step, here],
-                all_ss.at[step, off], all_rs.at[step, off], (lat_peer[off], lon),
-            )
-            for off in range(1, lat_n)
-        ]
+            rows_of.append(jnp.concatenate(pieces, 1))
+        return rows_of
 
     def send_partials(step, copies):
         for copy in copies:
             copy.wait_recv()
-        mass = mass_all[step]
+        mass = jnp.concatenate([part for band in range(lat_n) for part in band_of(step, band)], 0)
         both = [mass, turn(mass, ccols // 2, 1)]
         if jpad > jrows:
             blank = jnp.zeros((jpad - jrows, width), F32)
@@ -359,8 +372,8 @@
     loads[0].wait()
     loads[1].wait()
     field[4, :rows, :cols] = wet_in[...].astype(F32)
-    mass_copies = send_mass(0, field[0, :rows, :cols])
-    pending = list(mass_copies)
+    mass_copies, band_copies = send_mass(0, field[0, :rows, :cols])
+    pending = [copy for _, copy in mass_copies]
 
     for copy in loads[2:5]:
         copy.wait()
@@ -403,7 +416,7 @@
     for row in range(crows):
         put(row)
 
-    band_copies = send_band(0, mass_copies)
+    band_copies += send_band(0, mass_copies)
     pending += band_copies
 
     for copy in kh_copies:
@@ -493,16 +506,16 @@
         rowc, rises, state, False, lambda tile: None, lambda tile: None,
     )
 
-    mass_copies = send_mass(1, state[0, :rows, :cols])
+    mass_copies, band_copies = send_mass(1, state[0, :rows, :cols])
     prepare(1, state.at[0], state.at[1], state.at[2])
     keep(
         (ahead.at[1, 0], out_pack.at[3]),
         (ahead.at[1, 1], out_pack.at[4]),
         (state.at[0], out_pack.at[5]),
     )
-    band_copies = send_band(1, mass_copies)
+    band_copies += send_band(1, mass_copies)
     part_copies = send_partials(1, band_copies)
-    pending += mass_copies + band_copies + part_copies
+    pending += [copy for _, copy in mass_copies] + band_copies + part_copies
     out_loading[...] = loading_of(1, part_copies)
     for copy in pending:
         copy.wait_send()
@@ -517,7 +530,6 @@
     crows, ccols, jrows = kernel.shape
     all_rows, all_cols = rows + SUB, cols + LANES
     jpad = up(jrows, LANES)
-    width = up(ccols * lon_n + ccols + 1, LANES)
     square = up(rows, LANES)
     lags = 32 * ccols // 2
     dma = pltpu.SemaphoreType.DMA
@@ -544,8 +556,7 @@
             pltpu.VMEM((2 * jpad // LANES, lags, LANES), F32),
             pltpu.VMEM((lags, 2 * jpad), BF16),
             pltpu.VMEM((lags, 2 * jpad), BF16),
-            pltpu.VMEM((STEPS, lon_n, SUB, LANES), F32),
-            pltpu.VMEM((STEPS, jrows, width), F32),
+            pltpu.VMEM((STEPS, lat_n, lon_n, SUB, LANES), F32),
             pltpu.VMEM((STEPS, lon_n, SUB, LANES), F32),
             pltpu.VMEM((STEPS, lon_n, SUB, LANES), F32),
             pltpu.VMEM((2, 16, square), F32),
@@ -556,8 +567,8 @@
             dma((7,)),
             dma((STEPS, lon_n)),
             dma((STEPS, lon_n)),
-            dma((STEPS, lat_n)),
-            dma((STEPS, lat_n)),
+            dma((STEPS, lat_n, lon_n)),
+            dma((STEPS, lat_n, lon_n)),
             dma((STEPS, lon_n)),
             dma((STEPS, lon_n)),
             dma((2,)),

time: 35.5 us -> 36.4 us (1.025)
  Pallas kernels: 34.7 us -> 35.6 us
    pallas_call x1, Pallas kernels: 31.3 us -> 32.3 us  [body(): pl.pallas_call(functools.partial(run, lat_n, lon_n), out_shape=[pack, fac...]
where the time goes in v5:
time: 36.4 us; the launch traced here: 36.3 us
  Pallas kernels  35.6 us (98%)
  between operations  0.64 us (2%)
    pallas_call x1, Pallas kernels, body(): pl.pallas_call(functools.partial(run, lat_n, lon_n), out_shape=[pack, fac...  32.3 us
    pallas_call x1, Pallas kernels, body(): pl.pallas_call(finish, out_shape=[block, block, block, jax.ShapeDtypeStru...  3.36 us

profile of v5, /device:TPU:0, one launch (start us, length us, event | category | flops | bytes accessed | tf_op | source)
XLA Modules:
  0.0 36.3 jit_solution(6626506697671712695)
XLA Ops:
  0.6 32.3 %shard_map.93 = (f32[6,200,512]{2,1,0:T(8,128)}, f32[4,200,128]{2,1,0:T(8,128)}, f32[32,128]{1,0:T(8,128)}) custom-call(f32[192,384]{1,0:T(8,128)} %height.1, f32[192,384]{1,0:T(8,128)} %flux_lon.1, f32[192,384]{1,0:T(8,128)} %flux_lat.1, f32[192,384]{1,0:T(8,128)} %depth.1, s32[192,384]{1,0:T(8,128)} %wet.1, f32[24,24,96]{2,1,0:T(8,128)} %bitcast.1), custom_call_target="tpu_custom_call" | custom-call | tf_op jit(solution)/shard_map/pallas_call | solution.py:541
  32.9 3.4 %shard_map.94 = (f32[192,384]{1,0:T(8,128)}, f32[192,384]{1,0:T(8,128)}, f32[192,384]{1,0:T(8,128)}, f32[24,24]{1,0:T(8,128)}) custom-call(f32[6,200,512]{2,1,0:T(8,128)} %get-tuple-element.7.pack, f32[4,200,128]{2,1,0:T(8,128)} %get-tuple-element.8.rowc_in, f32[32,128]{1,0:T(8,128)} %get-tuple-element.9.loading_in), custom_call_target="tpu_custom_call" | custom-call | tf_op jit(solution)/shard_map/pallas_call | solution.py:585

commit v6 on v4

--- a/solution.py
+++ b/solution.py
@@ -345,9 +345,28 @@
             total = total + precv[step, off]
         return jnp.concatenate([turn(total, -32 * part, 1) for part in range(4)], 0)
 
-    def prepare(step, level, old_lon, old_lat):
+    def factors(which):
         sub = sub_of((SUB, all_cols))
-        for here in range(tiles):
+        for here in which:
+            at = pl.ds(here * SUB, SUB)
+            up_at = pl.ds((here + 1) % tiles * SUB, SUB)
+            deep, sea = field[3, at, :], field[4, at, :]
+            deep_north = turn(jnp.where(sub == 0, field[3, up_at, :], deep), SUB - 1, 0)
+            sea_north = turn(jnp.where(sub == 0, field[4, up_at, :], sea), SUB - 1, 0)
+            both = sea * turn(sea, all_cols - 1, 1)
+            coef[1, at, :] = both
+            coef[0, at, :] = (
+                both
+                * wide(rowc[1, at, :], all_cols // LANES)
+                * (0.5 * (deep + turn(deep, all_cols - 1, 1)))
+            )
+            both = sea * sea_north
+            coef[3, at, :] = both
+            coef[2, at, :] = both * (COURANT_LAT * 0.5) * (deep + deep_north)
+
+    def prepare(step, level, old_lon, old_lat, which):
+        sub = sub_of((SUB, all_cols))
+        for here in which:
             at = pl.ds(here * SUB, SUB)
             cells = level[at, :]
             after = level[pl.ds((here + 1) % tiles * SUB, SUB), :]
@@ -444,6 +463,8 @@
     part_copies = send_partials(0, band_copies)
     pending += part_copies
 
+    factors(range(tiles - 2))
+    prepare(0, field.at[0], field.at[1], field.at[2], range(tiles - 2))
     for copy in lath_copies:
         copy.wait_recv()
     for index in range(5):
@@ -455,23 +476,8 @@
             from_north = jnp.where(lat == lat_n - 1, 0.0, 1.0) * from_north
         field[index, rows:, :] = jnp.where(sub < SUB // 2, from_north, from_south)
 
-    for here in range(tiles):
-        at = pl.ds(here * SUB, SUB)
-        up_at = pl.ds((here + 1) % tiles * SUB, SUB)
-        deep, sea = field[3, at, :], field[4, at, :]
-        deep_north = turn(jnp.where(sub == 0, field[3, up_at, :], deep), SUB - 1, 0)
-        sea_north = turn(jnp.where(sub == 0, field[4, up_at, :], sea), SUB - 1, 0)
-        both = sea * turn(sea, all_cols - 1, 1)
-        coef[1, at, :] = both
-        coef[0, at, :] = (
-            both
-            * wide(rowc[1, at, :], all_cols // LANES)
-            * (0.5 * (deep + turn(deep, all_cols - 1, 1)))
-        )
-        both = sea * sea_north
-        coef[3, at, :] = both
-        coef[2, at, :] = both * (COURANT_LAT * 0.5) * (deep + deep_north)
-    prepare(0, field.at[0], field.at[1], field.at[2])
+    factors(range(tiles - 2, tiles))
+    prepare(0, field.at[0], field.at[1], field.at[2], range(tiles - 2, tiles))
 
     results = []
 
@@ -494,7 +500,7 @@
     )
 
     mass_copies = send_mass(1, state[0, :rows, :cols])
-    prepare(1, state.at[0], state.at[1], state.at[2])
+    prepare(1, state.at[0], state.at[1], state.at[2], range(tiles))
     keep(
         (ahead.at[1, 0], out_pack.at[3]),
         (ahead.at[1, 1], out_pack.at[4]),

time: 35.5 us -> 35.5 us (level)
  no operation moved by 1% of the time
where the time goes in v6:
time: 35.5 us; the launch traced here: 35.3 us
  Pallas kernels  34.7 us (98%)
  between operations  0.64 us (2%)
    pallas_call x1, Pallas kernels, body(): pl.pallas_call(functools.partial(run, lat_n, lon_n), out_shape=[pack, fac...  31.3 us
    pallas_call x1, Pallas kernels, body(): pl.pallas_call(finish, out_shape=[block, block, block, jax.ShapeDtypeStru...  3.36 us

profile of v6, /device:TPU:0, one launch (start us, length us, event | category | flops | bytes accessed | tf_op | source)
XLA Modules:
  0.0 35.3 jit_solution(2596282523160315545)
XLA Ops:
  0.6 31.3 %shard_map.93 = (f32[6,200,512]{2,1,0:T(8,128)}, f32[4,200,128]{2,1,0:T(8,128)}, f32[32,128]{1,0:T(8,128)}) custom-call(f32[192,384]{1,0:T(8,128)} %height.1, f32[192,384]{1,0:T(8,128)} %flux_lon.1, f32[192,384]{1,0:T(8,128)} %flux_lat.1, f32[192,384]{1,0:T(8,128)} %depth.1, s32[192,384]{1,0:T(8,128)} %wet.1, f32[24,24,96]{2,1,0:T(8,128)} %bitcast.1), custom_call_target="tpu_custom_call" | custom-call | tf_op jit(solution)/shard_map/pallas_call | solution.py:535
  32.0 3.4 %shard_map.94 = (f32[192,384]{1,0:T(8,128)}, f32[192,384]{1,0:T(8,128)}, f32[192,384]{1,0:T(8,128)}, f32[24,24]{1,0:T(8,128)}) custom-call(f32[6,200,512]{2,1,0:T(8,128)} %get-tuple-element.7.pack, f32[4,200,128]{2,1,0:T(8,128)} %get-tuple-element.8.rowc_in, f32[32,128]{1,0:T(8,128)} %get-tuple-element.9.loading_in), custom_call_target="tpu_custom_call" | custom-call | tf_op jit(solution)/shard_map/pallas_call | solution.py:580
